TPU v7x, 128 devices: a whole 4x4x4 slice. The times are simulated.
128 devices in a mesh: frame: 16 (over x, y), expert: 8 (over z, core).
Axes of the slice: x: 4, y: 4, z: 4, core: 2. Of those that a mesh axis runs over, the one named last changes fastest.
Arguments:
- patches: bfloat16 [16, 8, 256, 1536], P('frame', 'expert'), may hold values from -6 to 6
- temporal_q: bfloat16 [16, 8, 256, 1536], P('frame', 'expert'), may hold values from -70 to 70
- temporal_k: bfloat16 [16, 8, 256, 1536], P('frame', 'expert'), may hold values from -6 to 6
- temporal_v: bfloat16 [16, 8, 256, 1536], P('frame', 'expert'), may hold values from -6 to 6
- clip_lengths: int32 [8], P('expert'), may hold values from 1 to 16
- w_time: bfloat16 [1536, 1536], replicated, may hold values from -0.15625 to 0.15625
- gain_space: float32 [1536], replicated, may hold values from 0.1 to 1.9
- w_space: bfloat16 [1536, 4608], P(None, 'frame'), may hold values from -2 to 2
- w_merge: bfloat16 [1536, 1536], replicated, may hold values from -0.15625 to 0.15625
- gain_mix: float32 [1536], replicated, may hold values from 0.1 to 1.9
- expert_ids: int32 [16, 8, 256, 2], P('frame', 'expert'), may hold values from 0 to 31, all different within a row; in each aligned block of 256 rows (0 to 255, 256 to 511, ..., all dimensions but the last counted through in order) at most 18 rows name the same one
- gate_weights: float32 [16, 8, 256, 2], P('frame', 'expert'), may hold values from 0.25 to 1
- w_expand: bfloat16 [128, 1536, 1536], P(('frame', 'expert')), may hold values from -0.15625 to 0.15625
- w_reduce: bfloat16 [128, 1536, 1536], P(('frame', 'expert')), may hold values from -0.078125 to 0.078125
Outputs:
- block_out: bfloat16 [16, 8, 256, 1536], P('frame', 'expert')
Inputs may be any that keep to these rules, and one draw needn't show every extreme that they name: `expert_ids`: the rows of one device (the 256 rows of one frame and 1 clips) name no expert more than 18 times, and in some device's rows an expert is named exactly 18 times; the two experts of a row differ.
All inputs are finite; a program needn't handle non-finite values.
Results may differ from a plain program's by a relative error of at most 0.0065.
Values may be sent and summed in bfloat16 or wider, within the bound.
No kernel may reach another device: no remote copies, remote signals or barrier semaphores. Data moves between devices by JAX's collectives and lax.ppermute only.
A program may use at most 128 MiB of HBM per device.

v0:
```python
import math

import jax
import jax.numpy as jnp
from jax import lax
from jax.sharding import PartitionSpec as P

HEADS = 24
EXPERTS = 32
CAP = 18


epsilon = 1e-06


def layer_norm(values, gain_vector):
    centre = values - jnp.mean(values, axis=-1, keepdims=True)
    spread = jnp.mean(centre * centre, axis=-1, keepdims=True)
    return (centre * lax.rsqrt(spread + epsilon) * gain_vector).astype(jnp.bfloat16)


def softmax_rows(scores):
    top_score = jnp.max(scores, axis=-1, keepdims=True)
    powers = jnp.exp(scores - top_score)
    return (powers / jnp.sum(powers, axis=-1, keepdims=True)).astype(jnp.bfloat16)


def time_attention(queries, key_rows, value_rows, clip_lengths):
    frame_count, clip_count, place_count, model_width = queries.shape
    head_size = model_width // HEADS

    def split_heads(array_in):
        return array_in.reshape(frame_count, clip_count, place_count, HEADS, head_size)

    scores = jnp.einsum(
        "fcphd,gcphd->cphfg",
        split_heads(queries),
        split_heads(key_rows),
        preferred_element_type=jnp.float32,
    ) / math.sqrt(head_size)
    valid_keys = jnp.arange(frame_count, dtype=jnp.int32)[None, :] < clip_lengths[:, None]
    scores = jnp.where(valid_keys[:, None, None, None, :], scores, -1e30)
    weights = softmax_rows(scores)
    attended = jnp.einsum(
        "cphfg,gcphd->fcphd", weights, split_heads(value_rows), preferred_element_type=jnp.float32
    )
    return attended.astype(jnp.bfloat16).reshape(frame_count, clip_count, place_count, model_width)


def space_attention(projected):
    clip_count, place_count, triple = projected.shape
    model_width = triple // 3
    head_size = model_width // HEADS
    split_parts = projected.reshape(clip_count, place_count, 3, HEADS, head_size)
    scores = jnp.einsum(
        "cphd,cqhd->chpq",
        split_parts[:, :, 0],
        split_parts[:, :, 1],
        preferred_element_type=jnp.float32,
    ) / math.sqrt(head_size)
    weights = softmax_rows(scores)
    attended = jnp.einsum(
        "chpq,cqhd->cphd", weights, split_parts[:, :, 2], preferred_element_type=jnp.float32
    )
    return attended.astype(jnp.bfloat16).reshape(clip_count, place_count, model_width)


def expert_slots(routes):
    onehot = (routes[..., None] == jnp.arange(EXPERTS, dtype=jnp.int32)).astype(jnp.int32)
    earlier = jnp.cumsum(onehot, axis=-2) - onehot
    return jnp.sum(earlier * onehot, axis=-1)


def shards(
    patches,
    temporal_q,
    temporal_k,
    temporal_v,
    clip_lengths,
    w_time,
    gain_space,
    w_space,
    w_merge,
    gain_mix,
    expert_ids,
    gate_weights,
    w_expand,
    w_reduce,
):
    local_shape = patches.shape
    model_width = local_shape[-1]
    tube_q, tube_k, tube_v = (
        lax.all_to_all(temporal_q, "frame", split_axis=2, concat_axis=0, tiled=True),
        lax.all_to_all(temporal_k, "frame", split_axis=2, concat_axis=0, tiled=True),
        lax.all_to_all(temporal_v, "frame", split_axis=2, concat_axis=0, tiled=True),
    )
    tube_out = time_attention(tube_q, tube_k, tube_v, clip_lengths)
    time_mixed = lax.all_to_all(tube_out, "frame", split_axis=0, concat_axis=2, tiled=True)
    after_time = patches.astype(jnp.float32) + jnp.dot(
        time_mixed.reshape(-1, model_width), w_time, preferred_element_type=jnp.float32
    ).reshape(local_shape)
    normed = layer_norm(after_time, gain_space).reshape(-1, model_width)
    projected = jnp.dot(
        normed,
        lax.all_gather(w_space, "frame", axis=1, tiled=True),
        preferred_element_type=jnp.float32,
    ).astype(jnp.bfloat16)
    projected = projected.reshape(local_shape[0], local_shape[1], local_shape[2], 3 * model_width)
    spatial = lax.map(space_attention, projected)
    after_space = after_time + jnp.dot(
        spatial.reshape(-1, model_width), w_merge, preferred_element_type=jnp.float32
    ).reshape(local_shape)
    mixed_in = layer_norm(after_space, gain_mix).reshape(-1, model_width)
    row_count = mixed_in.shape[0]
    capacity = CAP
    routes = expert_ids.reshape(1, row_count * 2)
    slot_index = expert_slots(routes)[0]
    position = routes[0] * capacity + slot_index
    chosen = (position[:, None] == jnp.arange(EXPERTS * capacity, dtype=jnp.int32)[None, :]).astype(
        jnp.int32
    )
    chosen = jnp.sum(chosen.reshape(row_count, 2, EXPERTS * capacity), axis=1).astype(jnp.bfloat16)
    outgoing = jnp.einsum("re,rd->ed", chosen, mixed_in, preferred_element_type=jnp.float32).astype(
        jnp.bfloat16
    )
    outgoing = outgoing.reshape(EXPERTS, capacity, model_width)
    frame_size = lax.axis_size("frame")
    expert_size = lax.axis_size("expert")
    shard_count = frame_size * expert_size // EXPERTS
    expand_block = w_expand[0]
    reduce_block = w_reduce[0]
    replicas = jnp.repeat(outgoing, shard_count, axis=0)
    arrived = lax.all_to_all(replicas, ("frame", "expert"), split_axis=0, concat_axis=0, tiled=True)
    flat_rows = arrived.reshape(-1, model_width)
    hidden = jax.nn.gelu(
        jnp.dot(flat_rows, expand_block, preferred_element_type=jnp.float32), approximate=False
    ).astype(jnp.bfloat16)
    returned = lax.all_to_all(
        jnp.dot(hidden, reduce_block, preferred_element_type=jnp.float32)
        .astype(jnp.bfloat16)
        .reshape(arrived.shape),
        ("frame", "expert"),
        split_axis=0,
        concat_axis=0,
        tiled=True,
    )
    expert_table = jnp.sum(
        returned.reshape(EXPERTS, shard_count, capacity, model_width).astype(jnp.float32), axis=1
    )
    expert_table = expert_table.reshape(-1, model_width)
    picked = expert_table[position].reshape(row_count, 2, model_width)
    gate_rows = gate_weights.reshape(row_count, 2, 1)
    expert_mix = picked[:, 0] * gate_rows[:, 0] + picked[:, 1] * gate_rows[:, 1]
    return (after_space + expert_mix.reshape(local_shape)).astype(jnp.bfloat16)


def solution(mesh):
    return jax.shard_map(
        shards,
        mesh=mesh,
        in_specs=(
            P("frame", "expert", None, None),
            P("frame", "expert", None, None),
            P("frame", "expert", None, None),
            P("frame", "expert", None, None),
            P("expert"),
            P(),
            P(),
            P(None, "frame"),
            P(),
            P(),
            P("frame", "expert", None, None),
            P("frame", "expert", None, None),
            P(("frame", "expert"), None, None),
            P(("frame", "expert"), None, None),
        ),
        out_specs=P("frame", "expert", None, None),
        check_vma=False,
    )
```

profile of v0, /device:TPU:24, one launch (start us, length us, event | category | flops | bytes accessed | tf_op | source)
XLA Modules:
  0.0 532.1 jit_solution(8882313066790438491)
XLA Ops:
  10.1 5.4 %reduce.23 = bf16[256,1536]{1,0:T(8,128)(2,1)S(1)} reduce(bf16[256,1,1,1536]{3,2,1,0:T(2,128)(2,1)S(1)} %bitcast.130, bf16[]{:T(256)} %broadcast.225), dimensions={1,2}, to_apply=%bitcast.125.reduce_sub_computation | reduce | bytes 1572866
  17.0 7.5 %all-to-all-start = ((bf16[16,2,12288]{2,1,0:T(2,128)(2,1)}), bf16[16,2,12288]{2,1,0:T(2,128)(2,1)S(1)}, u32[]{:S(2)}, u32[]{:S(2)}) async-start(bf16[16,2,12288]{2,1,0:T(2,128)(2,1)} %reshape.488), calls=%async_computation | async-start | bytes 1572864 | tf_op jit(solution)/shard_map/all_to_all | solution.py:93
  26.9 5.4 %reduce.22 = bf16[256,1536]{1,0:T(8,128)(2,1)S(1)} reduce(bf16[256,1,1,1536]{3,2,1,0:T(2,128)(2,1)S(1)} %bitcast.132, bf16[]{:T(256)} %broadcast.225), dimensions={1,2}, to_apply=%bitcast.124.reduce_sub_computation | reduce | bytes 1572866
  33.8 11.7 %all-to-all-done = bf16[16,2,12288]{2,1,0:T(2,128)(2,1)S(1)} async-done(((bf16[16,2,12288]{2,1,0:T(2,128)(2,1)}), bf16[16,2,12288]{2,1,0:T(2,128)(2,1)S(1)}, u32[]{:S(2)}, u32[]{:S(2)}) %all-to-all-start) | async-done | bytes 786464 | tf_op jit(solution)/shard_map/all_to_all | solution.py:93
  45.5 6.7 %all-to-all-start.1 = ((bf16[16,2,12288]{2,1,0:T(2,128)(2,1)}), bf16[16,2,12288]{2,1,0:T(2,128)(2,1)}, u32[]{:S(2)}, u32[]{:S(2)}) async-start(bf16[16,2,12288]{2,1,0:T(2,128)(2,1)} %reshape.486), calls=%async_computation.1 | async-start | bytes 1572864 | tf_op jit(solution)/shard_map/all_to_all | solution.py:94
  54.5 5.4 %reduce.21 = bf16[256,1536]{1,0:T(8,128)(2,1)S(1)} reduce(bf16[256,1,1,1536]{3,2,1,0:T(2,128)(2,1)S(1)} %bitcast.131, bf16[]{:T(256)} %broadcast.225), dimensions={1,2}, to_apply=%bitcast.123.reduce_sub_computation | reduce | bytes 1572866
  61.7 4.5 all-to-all-done.1
  66.1 6.2 %all-to-all-start.2 = ((bf16[16,2,12288]{2,1,0:T(2,128)(2,1)}), bf16[16,2,12288]{2,1,0:T(2,128)(2,1)}, u32[]{:S(2)}, u32[]{:S(2)}) async-start(bf16[16,2,12288]{2,1,0:T(2,128)(2,1)} %reshape.484), calls=%async_computation.2 | async-start | bytes 1572864 | tf_op jit(solution)/shard_map/all_to_all | solution.py:95
  75.0 5.5 %bitcast_reduce_fusion = bf16[256,1536]{1,0:T(8,128)(2,1)} fusion(bf16[256,1,1,1536]{3,2,1,0:T(2,128)(2,1)S(1)} %reshape.489), kind=kLoop, calls=%fused_computation.134 | loop fusion | bytes 1572864 | tf_op jit(solution)/shard_map/all_to_all | solution.py:93
  87.3 5.5 %bitcast_reduce_fusion.1 = bf16[256,1536]{1,0:T(8,128)(2,1)} fusion(bf16[256,1,1,1536]{3,2,1,0:T(2,128)(2,1)S(1)} %reshape.487), kind=kLoop, calls=%fused_computation.135 | loop fusion | bytes 1572864 | tf_op jit(solution)/shard_map/all_to_all | solution.py:94
  95.9 4.6 reshape.485
  100.5 5.5 %bitcast_reduce_fusion.2 = bf16[256,1536]{1,0:T(8,128)(2,1)} fusion(bf16[256,1,1,1536]{3,2,1,0:T(2,128)(2,1)S(1)} %reshape.485), kind=kLoop, calls=%fused_computation.136 | loop fusion | bytes 1572864 | tf_op jit(solution)/shard_map/all_to_all | solution.py:95
  116.8 7.3 %all-to-all-start.3 = ((bf16[16,1,16,1536]{3,2,1,0:T(8,128)(2,1)}), bf16[16,1,16,1536]{3,2,1,0:T(8,128)(2,1)S(1)}, u32[]{:S(2)}, u32[]{:S(2)}) async-start(bf16[16,1,16,1536]{3,2,1,0:T(8,128)(2,1)} %bitcast.4), calls=%async_computation.3 | async-start | bytes 1572864 | tf_op jit(solution)/shard_map/all_to_all | solution.py:98
  125.6 10.7 %all-to-all-done.3 = bf16[16,1,16,1536]{3,2,1,0:T(8,128)(2,1)S(1)} async-done(((bf16[16,1,16,1536]{3,2,1,0:T(8,128)(2,1)}), bf16[16,1,16,1536]{3,2,1,0:T(8,128)(2,1)S(1)}, u32[]{:S(2)}, u32[]{:S(2)}) %all-to-all-start.3) | async-done | bytes 786464 | tf_op jit(solution)/shard_map/all_to_all | solution.py:98
  141.5 15.5 %convolution_convert_fusion.1 = bf16[256,4608]{1,0:T(8,128)(2,1)} fusion(bf16[1536,4608]{0,1:T(8,128)(2,1)} %all-gather.2.cloned.1.call-done, f32[1,1,256,1536]{3,2,1,0:T(8,128)S(1)} %get-tuple-element.21, f32[1536]{0:T(1024)S(1)} %copy-done.12, f32[256]{0:T(256)S(1)} %add_rsqrt_fusion.1, f32[256]{0:T(256)S(1)} %broadcast_multiply_fusion.2), kind=kOutput, calls=%fused_computation.24 | convolution fusion | flops 3626631168 | bytes 18096128 | tf_op jit(solution)/shard_map/dot_general | solution.py:103
  160.9 4.6 fusion.95
  174.5 118.9 %all_to_all.46 = bf16[128,18,1536]{2,1,0:T(8,128)(2,1)} all-to-all(bf16[128,18,1536]{2,1,0:T(8,128)(2,1)S(1)} %bitcast.127), channel_id=1, replica_groups=mesh['frame'=16,'expert'=8] {'frame','expert'}, dimensions={0} | all-to-all | bytes 14155776 | tf_op jit(solution)/shard_map/all_to_all | solution.py:133
  293.4 11.4 %reshape.466 = bf16[2304,1536]{1,0:T(8,128)(2,1)} reshape(bf16[128,18,1536]{2,1,0:T(8,128)(2,1)} %all_to_all.46) | data formatting | bytes 14155776 | tf_op jit(solution)/shard_map/reshape | solution.py:134
  304.7 41.9 %fusion.112 = bf16[2304,1536]{1,0:T(8,128)(2,1)S(1)} fusion(bf16[2304,1536]{1,0:T(8,128)(2,1)} %reshape.466, bf16[1,1536,1536]{2,1,0:T(8,128)(2,1)} %param.26), kind=kOutput, calls=%fused_computation.7.clone.clone.1 | convolution fusion | flops 11101667328 | bytes 18874368 | tf_op jit(solution)/shard_map/dot_general | solution.py:136
  346.6 12.9 %convolution_convert_fusion = bf16[2304,1536]{1,0:T(8,128)(2,1)} fusion(bf16[1,1536,1536]{2,1,0:T(8,128)(2,1)S(1)} %copy-done.11, bf16[2304,1536]{1,0:T(8,128)(2,1)S(1)} %fusion.112), kind=kOutput, calls=%fused_computation.23 | convolution fusion | flops 10875174912 | bytes 18874368 | tf_op jit(solution)/shard_map/dot_general | solution.py:139
  359.5 10.9 %reshape.467 = bf16[128,18,1536]{2,1,0:T(8,128)(2,1)} reshape(bf16[2304,1536]{1,0:T(8,128)(2,1)} %convolution_convert_fusion) | data formatting | bytes 14155776 | tf_op jit(solution)/shard_map/reshape | solution.py:141
  370.4 8.6 %all-to-all-start.5 = ((bf16[128,18,1536]{2,1,0:T(8,128)(2,1)}), bf16[128,18,1536]{2,1,0:T(8,128)(2,1)}, u32[]{:S(2)}, u32[]{:S(2)}) async-start(bf16[128,18,1536]{2,1,0:T(8,128)(2,1)} %reshape.467), calls=%async_computation.5 | async-start | bytes 18874368 | tf_op jit(solution)/shard_map/all_to_all | solution.py:138
  379.3 123.9 %all-to-all-done.5 = bf16[128,18,1536]{2,1,0:T(8,128)(2,1)} async-done(((bf16[128,18,1536]{2,1,0:T(8,128)(2,1)}), bf16[128,18,1536]{2,1,0:T(8,128)(2,1)}, u32[]{:S(2)}, u32[]{:S(2)}) %all-to-all-start.5) | async-done | bytes 7077920 | tf_op jit(solution)/shard_map/all_to_all | solution.py:138
  503.2 8.2 %convert_reduce_fusion = f32[32,18,1536]{2,1,0:T(8,128)} fusion(bf16[128,18,1536]{2,1,0:T(8,128)(2,1)} %all-to-all-done.5), kind=kLoop, calls=%fused_computation.4 | loop fusion | flops 6193152 | bytes 10616832 | tf_op jit(solution)/shard_map/reduce_sum | solution.py:147
  (93 shorter events, 68.7 us)
Async XLA Ops:
  6.5 134.2 %all-gather.2.cloned.1.call-start = ((), (), s32[]{:S(2)}) async-start(), calls=%async_computation.6 | async-start | bytes 15040512 | tf_op jit(solution)/shard_map/all_gather | solution.py:105
  17.0 28.5 %all-to-all-start = ((bf16[16,2,12288]{2,1,0:T(2,128)(2,1)}), bf16[16,2,12288]{2,1,0:T(2,128)(2,1)S(1)}, u32[]{:S(2)}, u32[]{:S(2)}) async-start(bf16[16,2,12288]{2,1,0:T(2,128)(2,1)} %reshape.488), calls=%async_computation | async-start | bytes 1572864 | tf_op jit(solution)/shard_map/all_to_all | solution.py:93
  32.3 29.1 %copy-start.9 = (s32[1,1,256,2]{2,3,1,0:T(2,128)S(1)}, s32[1,1,256,2]{2,3,1,0:T(2,128)}, u32[]{:S(2)}) copy-start(s32[1,1,256,2]{2,3,1,0:T(2,128)} %param.24) | copy-start | bytes 6148
  45.5 20.7 %all-to-all-start.1 = ((bf16[16,2,12288]{2,1,0:T(2,128)(2,1)}), bf16[16,2,12288]{2,1,0:T(2,128)(2,1)}, u32[]{:S(2)}, u32[]{:S(2)}) async-start(bf16[16,2,12288]{2,1,0:T(2,128)(2,1)} %reshape.486), calls=%async_computation.1 | async-start | bytes 1572864 | tf_op jit(solution)/shard_map/all_to_all | solution.py:94
  61.5 63.4 %copy-start.2 = (s32[1,1,256,2]{3,2,1,0:T(8,128)}, s32[1,1,256,2]{3,2,1,0:T(8,128)S(1)}, u32[]{:S(2)}) copy-start(s32[1,1,256,2]{3,2,1,0:T(8,128)S(1)} %copy.64) | copy-start | bytes 6148
  66.1 29.7 %all-to-all-start.2 = ((bf16[16,2,12288]{2,1,0:T(2,128)(2,1)}), bf16[16,2,12288]{2,1,0:T(2,128)(2,1)}, u32[]{:S(2)}, u32[]{:S(2)}) async-start(bf16[16,2,12288]{2,1,0:T(2,128)(2,1)} %reshape.484), calls=%async_computation.2 | async-start | bytes 1572864 | tf_op jit(solution)/shard_map/all_to_all | solution.py:95
  116.8 19.5 %all-to-all-start.3 = ((bf16[16,1,16,1536]{3,2,1,0:T(8,128)(2,1)}), bf16[16,1,16,1536]{3,2,1,0:T(8,128)(2,1)S(1)}, u32[]{:S(2)}, u32[]{:S(2)}) async-start(bf16[16,1,16,1536]{3,2,1,0:T(8,128)(2,1)} %bitcast.4), calls=%async_computation.3 | async-start | bytes 1572864 | tf_op jit(solution)/shard_map/all_to_all | solution.py:98
  124.7 0.6 copy-start.6
  136.3 5.2 copy-start.12
  140.3 1.2 copy-start.4
  160.8 5.4 %slice-start = ((s8[4718592]{0:T(1024)(128)(4,1)}), s8[4194304]{0:T(1024)(128)(4,1)S(1)}, s32[]{:S(2)}) async-start(s8[4718592]{0:T(1024)(128)(4,1)} %bitcast.143), calls=%async_computation.7 | async-start | bytes 8388608
  165.5 1.4 copy-start.5
  165.5 1.5 slice-start.1
  167.0 2.7 copy-start.8
  168.5 1.2 copy-start
  304.7 41.9 %copy-start.11 = (bf16[1,1536,1536]{2,1,0:T(8,128)(2,1)S(1)}, bf16[1,1536,1536]{2,1,0:T(8,128)(2,1)}, u32[]{:S(2)}) copy-start(bf16[1,1536,1536]{2,1,0:T(8,128)(2,1)} %param.27) | copy-start | bytes 14155780
  370.4 8.7 %copy-start.3 = (s32[1,1,256,2]{3,2,1,0:T(8,128)S(1)}, s32[1,1,256,2]{3,2,1,0:T(8,128)}, u32[]{:S(2)}) copy-start(s32[1,1,256,2]{3,2,1,0:T(8,128)} %copy-done.2) | copy-start | bytes 6148
  370.4 8.8 %copy-start.7 = (s32[512]{0:T(512)S(1)}, s32[512]{0:T(512)}, u32[]{:S(2)}) copy-start(s32[512]{0:T(512)} %copy-done.6) | copy-start | bytes 6148
  370.4 8.9 %copy-start.10 = (f32[1,1,256,2]{2,3,1,0:T(2,128)S(1)}, f32[1,1,256,2]{2,3,1,0:T(2,128)}, u32[]{:S(2)}) copy-start(f32[1,1,256,2]{2,3,1,0:T(2,128)} %param.25) | copy-start | bytes 6148
  370.4 132.8 %all-to-all-start.5 = ((bf16[128,18,1536]{2,1,0:T(8,128)(2,1)}), bf16[128,18,1536]{2,1,0:T(8,128)(2,1)}, u32[]{:S(2)}, u32[]{:S(2)}) async-start(bf16[128,18,1536]{2,1,0:T(8,128)(2,1)} %reshape.467), calls=%async_computation.5 | async-start | bytes 18874368 | tf_op jit(solution)/shard_map/all_to_all | solution.py:138
  521.4 2.4 copy-start.1
Sparse Core Ops, SparseCore 0:
  9.6 124.5 all-gather.1
where the time goes:
time: 539 us; the launch traced here: 532 us
  waiting for transfers between devices  151 us (28%)
  blocking collectives  119 us (22%)
  local copies, waits for them, and re-layouts  93.5 us (17%)
  matrix products  83 us (15%)
  starting transfers between devices  36.4 us (7%)
  other arithmetic  34.2 us (6%)
  between operations  14.7 us (3%)
    all_to_all x1, waiting for transfers between devices, shards(): lax.all_to_all(jnp.dot(hidden, reduce_block, preferred_element_type=jnp.f...  124 us
    all_to_all x1, blocking collectives, shards(): lax.all_to_all(replicas, ('frame', 'expert'), split_axis=0, concat_axis=0...  119 us
    dot_general x1, matrix products, shards(): jnp.dot(flat_rows, expand_block, preferred_element_type=jnp.float32)  41.9 us
    unnamed x41, local copies, waits for them, and re-layouts  24.6 us
    unnamed x4, other arithmetic  16.2 us
    dot_general x1, matrix products, shards(): jnp.dot(normed, lax.all_gather(w_space, 'frame', axis=1, tiled=True), pre...  15.5 us
    dot_general x1, matrix products, shards(): jnp.dot(hidden, reduce_block, preferred_element_type=jnp.float32)  12.9 us
    all_to_all x1, waiting for transfers between devices, shards(): lax.all_to_all(temporal_q, 'frame', split_axis=2, concat_axis=0, tiled=True)  11.7 us
  transfers between devices with their start and end apart: 6, of which 4 were waited for; matrix products, arithmetic and copies ran while one was open for 15% of the time, Pallas kernels for 0%

commit v1 on v0

v1 whole, which is shorter than its diff:
```python
import math

import jax
import jax.numpy as jnp
from jax import lax
from jax.experimental import pallas as pl
from jax.experimental.pallas import tpu as pltpu
from jax.sharding import Mesh, PartitionSpec as P

HEADS = 24
HEAD = 64
EXPERTS = 32
D = 1536
ROWS = 256
FRAMES = 16
MAIN = 16
PACK = 224
BLOCKS = D // 128
EPSILON = 1e-06
F32 = jnp.float32
BF16 = jnp.bfloat16
MIB = 1 << 20


def dot(a, b):
    return jnp.dot(a, b, preferred_element_type=F32)


def dot_nt(a, b):
    return lax.dot_general(a, b, (((1,), (1,)), ((), ())), preferred_element_type=F32)


def norm_rows(values, gain):
    centre = values - jnp.mean(values, axis=-1, keepdims=True)
    spread = jnp.mean(centre * centre, axis=-1, keepdims=True)
    return (centre * lax.rsqrt(spread + EPSILON) * gain).astype(BF16)


def time_kernel(len_ref, x_ref, o_ref):
    q = x_ref[:, 0:16, :].reshape(ROWS, 128)
    k = x_ref[:, 16:32, :].reshape(ROWS, 128)
    v = x_ref[:, 32:48, :].reshape(ROWS, 128)
    row = lax.broadcasted_iota(jnp.int32, (ROWS, ROWS), 0)
    col = lax.broadcasted_iota(jnp.int32, (ROWS, ROWS), 1)
    keep = ((row & 15) == (col & 15)) & ((col >> 4) < len_ref[0])
    low = lax.broadcasted_iota(jnp.int32, (ROWS, 128), 1) < HEAD
    zero = jnp.zeros((ROWS, 128), BF16)
    total = None
    for head in range(2):
        mine = low if head == 0 else ~low
        scores = dot_nt(q, jnp.where(mine, k, zero)) * (1.0 / math.sqrt(HEAD))
        scores = jnp.where(keep, scores, -1e30)
        powers = jnp.exp(scores - jnp.max(scores, axis=-1, keepdims=True))
        weights = (powers * (1.0 / jnp.sum(powers, axis=-1, keepdims=True))).astype(BF16)
        part = dot(weights, jnp.where(mine, v, zero))
        total = part if total is None else total + part
    o_ref[...] = total.astype(BF16).reshape(FRAMES, 16, 128)


def time_attention(lengths, qkv):
    return pl.pallas_call(
        time_kernel,
        grid=(BLOCKS,),
        in_specs=[
            pl.BlockSpec(memory_space=pltpu.SMEM),
            pl.BlockSpec((FRAMES, 48, 128), lambda i: (0, 0, i)),
        ],
        out_specs=pl.BlockSpec((FRAMES, 16, 128), lambda i: (0, 0, i)),
        out_shape=jax.ShapeDtypeStruct((FRAMES, 16, D), BF16),
        name="time_attention",
    )(lengths, qkv)


def after_time_kernel(mixed_ref, patch_ref, w_ref, gain_ref, after_ref, normed_ref):
    step = pl.program_id(0)
    cols = pl.ds(pl.multiple_of(step * 512, 512), 512)
    after_ref[:, cols] = patch_ref[...].astype(F32) + dot(mixed_ref[...], w_ref[...])

    @pl.when(step == 2)
    def _():
        normed_ref[...] = norm_rows(after_ref[...], gain_ref[...])


def after_time_step(mixed, patches, w_time, gain):
    return pl.pallas_call(
        after_time_kernel,
        grid=(3,),
        in_specs=[
            pl.BlockSpec((ROWS, D), lambda i: (0, 0)),
            pl.BlockSpec((ROWS, 512), lambda i: (0, i)),
            pl.BlockSpec((D, 512), lambda i: (0, i)),
            pl.BlockSpec((1, D), lambda i: (0, 0)),
        ],
        out_specs=[
            pl.BlockSpec((ROWS, D), lambda i: (0, 0)),
            pl.BlockSpec((ROWS, D), lambda i: (0, 0)),
        ],
        out_shape=[
            jax.ShapeDtypeStruct((ROWS, D), F32),
            jax.ShapeDtypeStruct((ROWS, D), BF16),
        ],
        name="after_time",
    )(mixed, patches, w_time, gain)


def spread_matrix():
    i = lax.broadcasted_iota(jnp.int32, (256, 192), 0)
    j = lax.broadcasted_iota(jnp.int32, (256, 192), 1)
    same = (i >> 5) == ((j & 15) >> 1)
    place = (i & 31) == 2 * (j >> 4) + (j & 1)
    return (same & place).astype(F32).astype(BF16)


def gather_matrix():
    j = lax.broadcasted_iota(jnp.int32, (192, 256), 0)
    i = lax.broadcasted_iota(jnp.int32, (192, 256), 1)
    same = (i >> 5) == ((j & 15) >> 1)
    place = (i & 31) == 2 * (j >> 4) + (j & 1)
    return (same & place).astype(F32).astype(BF16)


def unpack(block_ref, rows_ref):
    pick = gather_matrix()
    for j in range(BLOCKS):
        rows_ref[0:256, j * 128 : (j + 1) * 128] = block_ref[
            :, j * 16 : (j + 1) * 16, :
        ].reshape(256, 128)
    for half in range(2):
        packed = block_ref[half * 8 : (half + 1) * 8, 192:224, :].reshape(256, 128)
        last = dot(pick, packed).astype(BF16)
        for j in range(BLOCKS):
            rows_ref[256 + half * 16 : 272 + half * 16, j * 128 : (j + 1) * 128] = last[
                j * 16 : (j + 1) * 16, :
            ]


def space_kernel(
    normed_ref,
    w_ref,
    merge_ref,
    after_ref,
    gain_ref,
    main_ref,
    last_ref,
    space_ref,
    send_ref,
    projected,
    total,
):
    step = pl.program_id(0)

    @pl.when(step < FRAMES)
    def _():
        part = None
        for z in range(4):
            term = dot_nt(w_ref[0, z], normed_ref[:, z * 384 : (z + 1) * 384])
            part = term if part is None else part + term
        projected[pl.ds(pl.multiple_of(step * 288, 32), 288), :] = part.astype(BF16)

    @pl.when(step == FRAMES)
    def _():
        total[...] = after_ref[...]

    @pl.when(step >= FRAMES)
    def _():
        first = pl.multiple_of((step - FRAMES) * 128, 128)
        outs = []
        for head in range(2):
            base = first + head * HEAD
            q = projected[pl.ds(pl.multiple_of(base, 64), HEAD), :]
            k = projected[pl.ds(pl.multiple_of(base + D, 64), HEAD), :]
            v = projected[pl.ds(pl.multiple_of(base + 2 * D, 64), HEAD), :]
            scores = lax.dot_general(
                k, q, (((0,), (0,)), ((), ())), preferred_element_type=F32
            ) * (1.0 / math.sqrt(HEAD))
            powers = jnp.exp(scores - jnp.max(scores, axis=0, keepdims=True))
            weights = (powers * (1.0 / jnp.sum(powers, axis=0, keepdims=True))).astype(BF16)
            outs.append(dot(v, weights))
        both = jnp.concatenate(outs, axis=0).T.astype(BF16)
        total[...] += dot(both, merge_ref[...])

    @pl.when(step == FRAMES + BLOCKS - 1)
    def _():
        after_space = total[...]
        space_ref[...] = after_space
        mixed_in = norm_rows(after_space, gain_ref[...])
        slot = lax.broadcasted_iota(jnp.int32, (512, ROWS), 0)
        chosen = (slot == main_ref[0:1, :]) | (slot == main_ref[1:2, :])
        rows = dot(chosen.astype(F32).astype(BF16), mixed_in).astype(BF16)
        slot = lax.broadcasted_iota(jnp.int32, (64, ROWS), 0)
        chosen = (slot == last_ref[0:1, :]) | (slot == last_ref[1:2, :])
        last = dot(chosen.astype(F32).astype(BF16), mixed_in).astype(BF16)
        for j in range(BLOCKS):
            piece = rows[:, j * 128 : (j + 1) * 128].reshape(EXPERTS, 16, 128)
            for copy in range(2):
                send_ref[:, copy, j * 16 : (j + 1) * 16, :] = piece
        spread = spread_matrix()
        for group in range(4):
            own = last[group * 16 : (group + 1) * 16, :]
            tall = jnp.concatenate(
                [own[:, j * 128 : (j + 1) * 128] for j in range(BLOCKS)], axis=0
            )
            packed = dot(spread, tall).astype(BF16).reshape(8, 32, 128)
            for copy in range(2):
                send_ref[group * 8 : (group + 1) * 8, copy, 192:224, :] = packed


def space_step(normed, w_rows, w_merge, after_time, gain, main, last):
    whole = lambda i: (0, 0)
    return pl.pallas_call(
        space_kernel,
        grid=(FRAMES + BLOCKS,),
        in_specs=[
            pl.BlockSpec((ROWS, D), whole),
            pl.BlockSpec((1, 4, 288, 384), lambda i: (jnp.minimum(i, FRAMES - 1), 0, 0, 0)),
            pl.BlockSpec((128, D), lambda i: (jnp.maximum(i - FRAMES, 0), 0)),
            pl.BlockSpec((ROWS, D), whole),
            pl.BlockSpec((1, D), whole),
            pl.BlockSpec((2, ROWS), whole),
            pl.BlockSpec((2, ROWS), whole),
        ],
        out_specs=[
            pl.BlockSpec((ROWS, D), whole),
            pl.BlockSpec((EXPERTS, 2, PACK, 128), lambda i: (0, 0, 0, 0)),
        ],
        out_shape=[
            jax.ShapeDtypeStruct((ROWS, D), F32),
            jax.ShapeDtypeStruct((EXPERTS, 2, PACK, 128), BF16),
        ],
        scratch_shapes=[pltpu.VMEM((3 * D, ROWS), BF16), pltpu.VMEM((ROWS, D), F32)],
        compiler_params=pltpu.CompilerParams(vmem_limit_bytes=40 * MIB),
        name="space_attention",
    )(normed, w_rows, w_merge, after_time, gain, main, last)


CUT = 256
CUTS = D // CUT


def expert_kernel(with_sum, *refs):
    if with_sum:
        x_ref, other_ref, expand_hbm, reduce_hbm, o_ref = refs[:5]
    else:
        x_ref, expand_hbm, reduce_hbm, o_ref = refs[:4]
    expand, reduce, rows, hidden, sems = refs[-5:]
    step = pl.program_id(0)

    def fetch(n):
        cols = pl.ds((n % CUTS) * CUT, CUT)
        source, target = (expand_hbm, expand) if n < CUTS else (reduce_hbm, reduce)
        return pltpu.make_async_copy(source.at[0, :, cols], target.at[:, cols], sems.at[n])

    @pl.when(step == 0)
    def _():
        for n in range(2 * CUTS):
            fetch(n).start()

    unpack(x_ref, rows)
    for n in range(CUTS):

        @pl.when(step == 0)
        def _():
            fetch(n).wait()

        inner = dot(rows[...], expand[:, n * CUT : (n + 1) * CUT])
        active = inner * (0.5 + 0.5 * lax.erf(inner * math.sqrt(0.5)))
        hidden[:, n * CUT : (n + 1) * CUT] = active.astype(BF16)
    spread = spread_matrix()
    tops = [[], []]
    for n in range(CUTS):

        @pl.when(step == 0)
        def _():
            fetch(CUTS + n).wait()

        part = dot(hidden[...], reduce[:, n * CUT : (n + 1) * CUT])
        for j in range(CUT // 128):
            at = n * (CUT // 128) + j
            piece = part[:, j * 128 : (j + 1) * 128]
            main = piece[0:256].reshape(16, 16, 128)
            if with_sum:
                main = main + other_ref[:, at * 16 : (at + 1) * 16, :].astype(F32)
            o_ref[:, at * 16 : (at + 1) * 16, :] = main.astype(BF16)
            for half in range(2):
                tops[half].append(piece[256 + half * 16 : 272 + half * 16].astype(BF16))
    for half in range(2):
        packed = dot(spread, jnp.concatenate(tops[half], axis=0)).reshape(8, 32, 128)
        if with_sum:
            packed = packed + other_ref[half * 8 : (half + 1) * 8, 192:224, :].astype(F32)
        o_ref[half * 8 : (half + 1) * 8, 192:224, :] = packed.astype(BF16)


def run_experts(first, count, arrived, expand, reduce, other=None):
    block = (16, PACK, 128)
    from_first = pl.BlockSpec(block, lambda i: (i + first, 0, 0))
    from_zero = pl.BlockSpec(block, lambda i: (i, 0, 0))
    anywhere = pl.BlockSpec(memory_space=pl.ANY)
    more = [] if other is None else [other]

    def kernel(*refs):
        expert_kernel(other is not None, *refs)

    return pl.pallas_call(
        kernel,
        grid=(count,),
        in_specs=[from_first] + [from_zero] * len(more) + [anywhere, anywhere],
        out_specs=from_zero,
        out_shape=jax.ShapeDtypeStruct((16 * count, PACK, 128), BF16),
        scratch_shapes=[
            pltpu.VMEM((D, D), BF16),
            pltpu.VMEM((D, D), BF16),
            pltpu.VMEM((288, D), BF16),
            pltpu.VMEM((288, D), BF16),
            pltpu.SemaphoreType.DMA((2 * CUTS,)),
        ],
        compiler_params=pltpu.CompilerParams(vmem_limit_bytes=40 * MIB),
        cost_estimate=pl.CostEstimate(
            flops=count * 288 * D * D * 4,
            bytes_accessed=4 * D * D + count * 32 * PACK * 128 * 2,
            transcendentals=count * 288 * D,
        ),
        name="experts",
    )(arrived, *more, expand, reduce)


def combine_kernel(x_ref, main_ref, last_ref, gate_ref, space_ref, o_ref, rows, totals):
    step = pl.program_id(0)

    @pl.when(step == 0)
    def _():
        totals[...] = jnp.zeros_like(totals)

    unpack(x_ref, rows)
    at = lax.broadcasted_iota(jnp.int32, (ROWS, 288), 1)
    in_last = at >= 256
    expert = jnp.where(in_last, (at - 256) >> 2, at >> 5) + step * 8
    code = jnp.where(in_last, expert * 2 + (at & 1), expert * 16 + (at & 15))
    for k in range(2):
        wanted = jnp.where(in_last, last_ref[:, k : k + 1], main_ref[:, k : k + 1])
        totals[k] += dot((code == wanted).astype(F32).astype(BF16), rows[...])

    @pl.when(step == 3)
    def _():
        mix = totals[0] * gate_ref[:, 0:1] + totals[1] * gate_ref[:, 1:2]
        o_ref[...] = (space_ref[...] + mix).astype(BF16)


def combine(returned, main, last, gates, after_space):
    whole = lambda i: (0, 0)
    return pl.pallas_call(
        combine_kernel,
        grid=(4,),
        in_specs=[
            pl.BlockSpec((16, PACK, 128), lambda i: (i, 0, 0)),
            pl.BlockSpec((ROWS, 2), whole),
            pl.BlockSpec((ROWS, 2), whole),
            pl.BlockSpec((ROWS, 2), whole),
            pl.BlockSpec((ROWS, D), whole),
        ],
        out_specs=pl.BlockSpec((ROWS, D), whole),
        out_shape=jax.ShapeDtypeStruct((ROWS, D), BF16),
        scratch_shapes=[pltpu.VMEM((288, D), BF16), pltpu.VMEM((2, ROWS, D), F32)],
        compiler_params=pltpu.CompilerParams(vmem_limit_bytes=40 * MIB),
        name="combine",
    )(returned, main, last, gates, after_space)


def shards(
    patches,
    temporal_q,
    temporal_k,
    temporal_v,
    clip_lengths,
    w_time,
    gain_space,
    w_space,
    w_merge,
    gain_mix,
    expert_ids,
    gate_weights,
    w_expand,
    w_reduce,
):
    frame_axes, chip_axes = ("x", "y"), ("x", "y", "z")
    swap = [(0, 1), (1, 0)]

    own_rows = lax.dynamic_slice(
        w_space,
        (lax.axis_index("z") * 384, lax.axis_index("c") * 144),
        (384, 144),
    ).T
    w_rows = lax.all_gather(own_rows, ("x", "y", "z", "c"), axis=0, tiled=True)
    w_rows = w_rows.reshape(FRAMES, 4, 288, 384)

    qkv = jnp.concatenate(
        [a.reshape(FRAMES, 16, D) for a in (temporal_q, temporal_k, temporal_v)], axis=1
    )
    qkv = lax.all_to_all(qkv, frame_axes, split_axis=0, concat_axis=0, tiled=True)
    mixed = time_attention(clip_lengths, qkv)
    mixed = lax.all_to_all(mixed, frame_axes, split_axis=0, concat_axis=0, tiled=True)
    after_time, normed = after_time_step(
        mixed.reshape(ROWS, D), patches.reshape(ROWS, D), w_time, gain_space.reshape(1, D)
    )

    experts = expert_ids.reshape(ROWS * 2)
    index = jnp.arange(ROWS * 2, dtype=jnp.int32)
    earlier = (experts[:, None] == experts[None, :]) & (index[None, :] < index[:, None])
    slot = jnp.sum(earlier.astype(jnp.int32), axis=1)
    main = jnp.where(slot < MAIN, experts * MAIN + slot, -1).reshape(ROWS, 2)
    last = jnp.where(slot >= MAIN, experts * 2 + slot - MAIN, -1).reshape(ROWS, 2)

    after_space, outgoing = space_step(
        normed, w_rows, w_merge, after_time, gain_mix.reshape(1, D), main.T, last.T
    )
    arrived = lax.all_to_all(
        outgoing.reshape(64, PACK, 128), chip_axes, split_axis=0, concat_axis=0, tiled=True
    )
    theirs = lax.ppermute(arrived, "c", swap)
    part_own = run_experts(0, 2, arrived, w_expand, w_reduce)
    part_a = run_experts(0, 2, theirs, w_expand, w_reduce)
    back_a = lax.ppermute(part_a, "c", swap)
    part_b = run_experts(2, 2, theirs, w_expand, w_reduce)
    back_b = lax.ppermute(part_b, "c", swap)
    sum_a = (part_own.astype(F32) + back_a.astype(F32)).astype(BF16)
    sum_b = run_experts(2, 2, arrived, w_expand, w_reduce, back_b)
    returned = lax.all_to_all(
        jnp.concatenate([sum_a, sum_b], axis=0), chip_axes, split_axis=0, concat_axis=0, tiled=True
    )
    out = combine(returned, main, last, gate_weights.reshape(ROWS, 2), after_space)
    return out.reshape(patches.shape)


def solution(mesh):
    grid = Mesh(mesh.devices.reshape(4, 4, 4, 2), ("x", "y", "z", "c"))
    frame, clip = ("x", "y"), ("z", "c")
    every = ("x", "y", "z", "c")
    return jax.shard_map(
        shards,
        mesh=grid,
        in_specs=(
            P(frame, clip, None, None),
            P(frame, clip, None, None),
            P(frame, clip, None, None),
            P(frame, clip, None, None),
            P(clip),
            P(),
            P(),
            P(None, frame),
            P(),
            P(),
            P(frame, clip, None, None),
            P(frame, clip, None, None),
            P(every, None, None),
            P(every, None, None),
        ),
        out_specs=P(frame, clip, None, None),
        check_vma=False,
    )
```

time: 539 us -> 350 us (0.65)
  the two profiles are of different devices: /device:TPU:24 before, /device:TPU:82 now
where the time goes in v1:
time: 350 us; the launch traced here: 348 us
  Pallas kernels  119 us (34%)
  waiting for transfers between devices  113 us (32%)
  blocking collectives  52.4 us (15%)
  starting transfers between devices  26.6 us (8%)
  local copies, waits for them, and re-layouts  16.5 us (5%)
  between operations  14.2 us (4%)
  other arithmetic  6.1 us (2%)
    pallas_call x4, Pallas kernels, run_experts(): pl.pallas_call(kernel, grid=(count,), in_specs=[from_first] + [from_zero]...  64.7 us
    all_to_all x1, blocking collectives, shards(): lax.all_to_all(outgoing.reshape(64, PACK, 128), chip_axes, split_axis=0,...  52.4 us
    all_to_all x1, waiting for transfers between devices, shards(): lax.all_to_all(jnp.concatenate([sum_a, sum_b], axis=0), chip_axes, split_...  50.7 us
    pallas_call x1, Pallas kernels, space_step(): pl.pallas_call(space_kernel, grid=(FRAMES + BLOCKS,), in_specs=[pl.BlockS...  30.3 us
    all_to_all x1, waiting for transfers between devices, shards(): lax.all_to_all(qkv, frame_axes, split_axis=0, concat_axis=0, tiled=True)  29.8 us
    all_gather x1, waiting for transfers between devices, shards(): w_rows = lax.all_gather(own_rows, ('x', 'y', 'z', 'c'), axis=0, tiled=True)  18.4 us
    unnamed x34, local copies, waits for them, and re-layouts  14.8 us
    all_to_all x1, starting transfers between devices, shards(): lax.all_to_all(jnp.concatenate([sum_a, sum_b], axis=0), chip_axes, split_...  10.4 us
  transfers between devices with their start and end apart: 7, of which 5 were waited for; matrix products, arithmetic and copies ran while one was open for 1% of the time, Pallas kernels for 19%

profile of v1, /device:TPU:82, one launch (start us, length us, event | category | flops | bytes accessed | tf_op | source)
XLA Modules:
  0.0 348.3 jit_solution(7467373248719219419)
XLA Ops:
  8.4 3.2 pad_maximum_fusion.1
  11.6 7.4 %all-to-all-start = ((bf16[16,48,1536]{2,1,0:T(8,128)(2,1)}), bf16[16,48,1536]{2,1,0:T(8,128)(2,1)S(1)}, u32[]{:S(2)}, u32[]{:S(2)}) async-start(bf16[16,48,1536]{2,1,0:T(8,128)(2,1)} %pad_maximum_fusion.1), calls=%async_computation | async-start | bytes 4718592 | tf_op jit(solution)/shard_map/all_to_all | solution.py:398
  19.6 29.8 %all-to-all-done.x_ref = bf16[16,48,1536]{2,1,0:T(8,128)(2,1)S(1)} async-done(((bf16[16,48,1536]{2,1,0:T(8,128)(2,1)}), bf16[16,48,1536]{2,1,0:T(8,128)(2,1)S(1)}, u32[]{:S(2)}, u32[]{:S(2)}) %all-to-all-start) | async-done | bytes 2359328 | tf_op jit(solution)/shard_map/all_to_all | solution.py:398
  50.8 10.4 %time_attention.1 = bf16[16,16,1536]{2,1,0:T(8,128)(2,1)} custom-call(s32[1]{0:T(128)S(6)} %copy.32.len_ref, bf16[16,48,1536]{2,1,0:T(8,128)(2,1)} %copy-done.8), custom_call_target="tpu_custom_call" | custom-call | tf_op jit(solution)/shard_map/time_attention/pallas_call | solution.py:61
  61.1 8.0 %all-to-all-start.1 = ((bf16[16,16,1536]{2,1,0:T(8,128)(2,1)}), bf16[16,16,1536]{2,1,0:T(8,128)(2,1)S(1)}, u32[]{:S(2)}, u32[]{:S(2)}) async-start(bf16[16,16,1536]{2,1,0:T(8,128)(2,1)} %time_attention.1), calls=%async_computation.1 | async-start | bytes 1572864 | tf_op jit(solution)/shard_map/all_to_all | solution.py:400
  70.7 8.1 %all-to-all-done.1 = bf16[16,16,1536]{2,1,0:T(8,128)(2,1)S(1)} async-done(((bf16[16,16,1536]{2,1,0:T(8,128)(2,1)}), bf16[16,16,1536]{2,1,0:T(8,128)(2,1)S(1)}, u32[]{:S(2)}, u32[]{:S(2)}) %all-to-all-start.1) | async-done | bytes 786464 | tf_op jit(solution)/shard_map/all_to_all | solution.py:400
  79.6 6.8 %after_time.1 = (f32[256,1536]{1,0:T(8,128)}, bf16[256,1536]{1,0:T(8,128)(2,1)}) custom-call(bf16[256,1536]{1,0:T(8,128)(2,1)} %bitcast.32, bf16[256,1536]{1,0:T(8,128)(2,1)} %bitcast.36, bf16[1536,1536]{1,0:T(8,128)(2,1)} %w_ref.1, f32[1,1536]{1,0:T(1,128)} %reshape.51.gain_ref), custom_call_target="tpu_custom_call" | custom-call | tf_op jit(solution)/shard_map/after_time/pallas_call | solution.py:85
  86.4 18.4 %all-gather.2.cloned.1.call-done = bf16[18432,384]{1,0:T(8,128)(2,1)} async-done(((bf16[144,384]{1,0:T(8,128)(2,1)}), bf16[18432,384]{1,0:T(8,128)(2,1)}) %all-gather.2.cloned.1.call-update) | async-done | bytes 14155792 | tf_op jit(solution)/shard_map/all_gather | solution.py:392
  104.8 2.3 copy-done.2
  107.1 1.4 copy-done.3
  109.6 30.3 %space_attention.1 = (f32[256,1536]{1,0:T(8,128)S(1)}, bf16[32,2,224,128]{3,2,1,0:T(8,128)(2,1)S(1)}) custom-call(bf16[256,1536]{1,0:T(8,128)(2,1)S(1)} %copy-done.4, bf16[16,4,288,384]{3,2,1,0:T(8,128)(2,1)} %bitcast.31, bf16[1536,1536]{1,0:T(8,128)(2,1)S(1)} %copy-done.2, f32[256,1536]{1,0:T(8,128)S(1)} %copy-done.3, f32[1,1536]{1,0:T(1,128)S(1)} %reshape.53.gain_ref, ...), custom_call_target="tpu_custom_call" | custom-call | tf_op jit(solution)/shard_map/space_attention/pallas_call | solution.py:210
  139.9 52.4 %all_to_all.20.refs_0_ = bf16[64,224,128]{2,1,0:T(8,128)(2,1)S(1)} all-to-all(bf16[64,224,128]{2,1,0:T(8,128)(2,1)S(1)} %bitcast.25), channel_id=1, replica_groups=mesh['x'=4,'y'=4,'z'=4,'c'=2] {'x','y','z'}, dimensions={0} | all-to-all | bytes 7340032 | tf_op jit(solution)/shard_map/all_to_all | solution.py:415
  192.2 6.4 %collective-permute-done.refs_0_ = bf16[64,224,128]{2,1,0:T(8,128)(2,1)S(1)} collective-permute-done((bf16[64,224,128]{2,1,0:T(8,128)(2,1)S(1)}, bf16[64,224,128]{2,1,0:T(8,128)(2,1)S(1)}, u32[]{:S(2)}, u32[]{:S(2)}) %collective-permute-start) | collective-permute-done | bytes 3670048 | tf_op jit(solution)/shard_map/ppermute | solution.py:418
  198.7 1.8 copy-done.6
  200.4 2.3 copy-done.5
  202.8 2.0 copy-done.7
  204.8 16.2 %experts.6 = bf16[32,224,128]{2,1,0:T(8,128)(2,1)S(1)} custom-call(bf16[64,224,128]{2,1,0:T(8,128)(2,1)S(1)} %copy-done.7, bf16[1,1536,1536]{2,1,0:T(8,128)(2,1)S(1)} %copy-done.5, bf16[1,1536,1536]{2,1,0:T(8,128)(2,1)} %refs_3_.1), custom_call_target="tpu_custom_call" | custom-call | flops 5435817984 | bytes 13107200 | tf_op jit(solution)/shard_map/experts/pallas_call | solution.py:303
  221.4 16.2 %experts.5 = bf16[32,224,128]{2,1,0:T(8,128)(2,1)S(1)} custom-call(bf16[64,224,128]{2,1,0:T(8,128)(2,1)S(1)} %copy-done.7, bf16[1,1536,1536]{2,1,0:T(8,128)(2,1)S(1)} %copy-done.5, bf16[1,1536,1536]{2,1,0:T(8,128)(2,1)} %refs_3_.1), custom_call_target="tpu_custom_call" | custom-call | flops 5435817984 | bytes 13107200 | tf_op jit(solution)/shard_map/experts/pallas_call | solution.py:303
  238.0 16.2 %experts.4 = bf16[32,224,128]{2,1,0:T(8,128)(2,1)S(1)} custom-call(bf16[64,224,128]{2,1,0:T(8,128)(2,1)S(1)} %all_to_all.20.refs_0_, bf16[1,1536,1536]{2,1,0:T(8,128)(2,1)S(1)} %bitcast.30, bf16[1,1536,1536]{2,1,0:T(8,128)(2,1)} %refs_3_.1), custom_call_target="tpu_custom_call" | custom-call | flops 5435817984 | bytes 13107200 | tf_op jit(solution)/shard_map/experts/pallas_call | solution.py:303
  254.2 16.2 %experts.7 = bf16[32,224,128]{2,1,0:T(8,128)(2,1)S(1)} custom-call(bf16[64,224,128]{2,1,0:T(8,128)(2,1)S(1)} %all_to_all.20.refs_0_, bf16[32,224,128]{2,1,0:T(8,128)(2,1)S(1)} %collective-permute-done.2.refs_1_, bf16[1,1536,1536]{2,1,0:T(8,128)(2,1)S(1)} %bitcast.30, bf16[1,1536,1536]{2,1,0:T(8,128)(2,1)} %refs_3_.1), custom_call_target="tpu_custom_call" | custom-call | flops 5435817984 | bytes 13107200 | tf_op jit(solution)/shard_map/experts/pallas_call | solution.py:303
  270.9 2.1 pad_maximum_fusion
  273.1 10.4 %all-to-all-start.3 = ((bf16[64,224,128]{2,1,0:T(8,128)(2,1)}), bf16[64,224,128]{2,1,0:T(8,128)(2,1)}, u32[]{:S(2)}, u32[]{:S(2)}) async-start(bf16[64,224,128]{2,1,0:T(8,128)(2,1)} %pad_maximum_fusion), calls=%async_computation.3 | async-start | bytes 7340032 | tf_op jit(solution)/shard_map/all_to_all | solution.py:426
  283.7 50.7 %all-to-all-done.3.x_ref = bf16[64,224,128]{2,1,0:T(8,128)(2,1)} async-done(((bf16[64,224,128]{2,1,0:T(8,128)(2,1)}), bf16[64,224,128]{2,1,0:T(8,128)(2,1)}, u32[]{:S(2)}, u32[]{:S(2)}) %all-to-all-start.3) | async-done | bytes 3670048 | tf_op jit(solution)/shard_map/all_to_all | solution.py:426
  334.4 7.1 %combine.1 = bf16[256,1536]{1,0:T(8,128)(2,1)} custom-call(bf16[64,224,128]{2,1,0:T(8,128)(2,1)} %all-to-all-done.3.x_ref, s32[256,2]{1,0:T(8,128)S(1)} %get-tuple-element.14.main_ref, s32[256,2]{1,0:T(8,128)S(1)} %get-tuple-element.13.last_ref, f32[256,2]{1,0:T(8,128)S(1)} %bitcast.28, f32[256,1536]{1,0:T(8,128)S(1)} %get-tuple-element.12.space_ref), custom_call_target="tpu_custom_call" | custom-call | tf_op jit(solution)/shard_map/combine/pallas_call | solution.py:350
  (47 shorter events, 8.2 us)
Async XLA Ops:
  6.5 1.2 copy-start
  6.5 98.2 %all-gather.2.cloned.1.call-start = ((), (), s32[]{:S(2)}) async-start(), calls=%async_computation.4 | async-start | bytes 14266368 | tf_op jit(solution)/shard_map/all_gather | solution.py:392
  11.6 57.6 %copy-start.12 = (s32[1,1,256,2]{2,3,1,0:T(2,128)S(1)}, s32[1,1,256,2]{2,3,1,0:T(2,128)}, u32[]{:S(2)}) copy-start(s32[1,1,256,2]{2,3,1,0:T(2,128)} %param.24) | copy-start | bytes 6148
  11.6 37.8 %all-to-all-start = ((bf16[16,48,1536]{2,1,0:T(8,128)(2,1)}), bf16[16,48,1536]{2,1,0:T(8,128)(2,1)S(1)}, u32[]{:S(2)}, u32[]{:S(2)}) async-start(bf16[16,48,1536]{2,1,0:T(8,128)(2,1)} %pad_maximum_fusion.1), calls=%async_computation | async-start | bytes 4718592 | tf_op jit(solution)/shard_map/all_to_all | solution.py:398
  18.9 51.1 %copy-start.10 = (f32[1536]{0:T(1024)S(1)}, f32[1536]{0:T(1024)}, u32[]{:S(2)}) copy-start(f32[1536]{0:T(1024)} %param.20) | copy-start | bytes 18436
  18.9 51.7 %copy-start.11 = (f32[1536]{0:T(1024)S(1)}, f32[1536]{0:T(1024)}, u32[]{:S(2)}) copy-start(f32[1536]{0:T(1024)} %param.23) | copy-start | bytes 18436
  49.4 1.4 copy-start.8
  61.1 17.6 %all-to-all-start.1 = ((bf16[16,16,1536]{2,1,0:T(8,128)(2,1)}), bf16[16,16,1536]{2,1,0:T(8,128)(2,1)S(1)}, u32[]{:S(2)}, u32[]{:S(2)}) async-start(bf16[16,16,1536]{2,1,0:T(8,128)(2,1)} %time_attention.1), calls=%async_computation.1 | async-start | bytes 1572864 | tf_op jit(solution)/shard_map/all_to_all | solution.py:400
  78.7 0.9 copy-start.9
  104.7 2.3 copy-start.2
  107.1 1.4 copy-start.3
  108.5 1.1 copy-start.4
  192.2 6.4 %collective-permute-start = (bf16[64,224,128]{2,1,0:T(8,128)(2,1)S(1)}, bf16[64,224,128]{2,1,0:T(8,128)(2,1)S(1)}, u32[]{:S(2)}, u32[]{:S(2)}) collective-permute-start(bf16[64,224,128]{2,1,0:T(8,128)(2,1)S(1)} %all_to_all.20.refs_0_), channel_id=1, source_target_pairs={{0,1},{1,0},{2,3},{3,2},{4,5},{5,4},{6,7},{7,6},{8,9},{9,8},{10,11... | collective-permute-start | bytes 11010056 | tf_op jit(solution)/shard_map/ppermute | solution.py:418
  198.7 1.8 copy-start.6
  200.4 2.3 copy-start.5
  202.8 2.0 copy-start.7
  204.8 33.2 %slice-start = ((s8[4718592]{0:T(1024)(128)(4,1)}), s8[4194304]{0:T(1024)(128)(4,1)S(1)}, s32[]{:S(2)}) async-start(s8[4718592]{0:T(1024)(128)(4,1)} %bitcast.29), calls=%async_computation.5 | async-start | bytes 8388608
  221.0 17.1 %slice-start.1 = ((s8[4718592]{0:T(1024)(128)(4,1)}), s8[524288]{0:T(1024)(128)(4,1)S(1)}, s32[]{:S(2)}) async-start(s8[4718592]{0:T(1024)(128)(4,1)} %bitcast.29), calls=%async_computation.6 | async-start | bytes 1048576
  221.0 33.2 %collective-permute-start.2 = (bf16[32,224,128]{2,1,0:T(8,128)(2,1)S(1)}, bf16[32,224,128]{2,1,0:T(8,128)(2,1)S(1)}, u32[]{:S(2)}, u32[]{:S(2)}) collective-permute-start(bf16[32,224,128]{2,1,0:T(8,128)(2,1)S(1)} %experts.6), channel_id=1, source_target_pairs={{0,1},{1,0},{2,3},{3,2},{4,5},{5,4},{6,7},{7,6},{8,9},{9,8},{10,11... | collective-permute-start | bytes 5505032 | tf_op jit(solution)/shard_map/ppermute | solution.py:423
  237.6 32.9 %collective-permute-start.1 = (bf16[32,224,128]{2,1,0:T(8,128)(2,1)S(1)}, bf16[32,224,128]{2,1,0:T(8,128)(2,1)S(1)}, u32[]{:S(2)}, u32[]{:S(2)}) collective-permute-start(bf16[32,224,128]{2,1,0:T(8,128)(2,1)S(1)} %experts.5), channel_id=1, source_target_pairs={{0,1},{1,0},{2,3},{3,2},{4,5},{5,4},{6,7},{7,6},{8,9},{9,8},{10,11... | collective-permute-start | bytes 5505032 | tf_op jit(solution)/shard_map/ppermute | solution.py:421
  273.1 10.5 %copy-start.13 = (f32[1,1,256,2]{2,3,1,0:T(2,128)S(1)}, f32[1,1,256,2]{2,3,1,0:T(2,128)}, u32[]{:S(2)}) copy-start(f32[1,1,256,2]{2,3,1,0:T(2,128)} %param.25) | copy-start | bytes 6148
  273.1 61.3 %all-to-all-start.3 = ((bf16[64,224,128]{2,1,0:T(8,128)(2,1)}), bf16[64,224,128]{2,1,0:T(8,128)(2,1)}, u32[]{:S(2)}, u32[]{:S(2)}) async-start(bf16[64,224,128]{2,1,0:T(8,128)(2,1)} %pad_maximum_fusion), calls=%async_computation.3 | async-start | bytes 7340032 | tf_op jit(solution)/shard_map/all_to_all | solution.py:426
  283.5 57.9 %copy-start.1 = (bf16[1536,288]{0,1:T(8,128)(2,1)S(1)}, bf16[1536,288]{0,1:T(8,128)(2,1)}, u32[]{:S(2)}) copy-start(bf16[1536,288]{0,1:T(8,128)(2,1)} %param.21) | copy-start | bytes 2654212
Sparse Core Ops, SparseCore 0:
  10.4 94.3 all-gather.1

commit v2 on v1

v2 whole, which is shorter than its diff:
```python
import math

import jax
import jax.numpy as jnp
from jax import lax
from jax.experimental import pallas as pl
from jax.experimental.pallas import tpu as pltpu
from jax.sharding import Mesh, PartitionSpec as P

HEADS = 24
HEAD = 64
EXPERTS = 32
D = 1536
ROWS = 256
FRAMES = 16
MAIN = 16
PACK = 224
BLOCKS = D // 128
EPSILON = 1e-06
F32 = jnp.float32
BF16 = jnp.bfloat16
VMEM = 40 << 20


def dot(a, b):
    return jnp.dot(a, b, preferred_element_type=F32)


def dot_nt(a, b):
    return lax.dot_general(a, b, (((1,), (1,)), ((), ())), preferred_element_type=F32)


def in_vmem(array):
    return pltpu.with_memory_space_constraint(array, pltpu.VMEM)


def in_hbm(array):
    return pltpu.with_memory_space_constraint(array, pltpu.HBM)


def norm_rows(values, gain):
    centre = values - jnp.mean(values, axis=-1, keepdims=True)
    spread = jnp.mean(centre * centre, axis=-1, keepdims=True)
    return (centre * lax.rsqrt(spread + EPSILON) * gain).astype(BF16)


TIME_PAIRS = 3


def time_kernel(len_ref, x_ref, o_ref):
    row = lax.broadcasted_iota(jnp.int32, (ROWS, ROWS), 0)
    col = lax.broadcasted_iota(jnp.int32, (ROWS, ROWS), 1)
    keep = ((row & 15) == (col & 15)) & ((col >> 4) < len_ref[0])
    low = lax.broadcasted_iota(jnp.int32, (ROWS, 128), 1) < HEAD
    zero = jnp.zeros((ROWS, 128), BF16)
    def heads(step, carry):
        for pair in range(TIME_PAIRS):
            lanes = pl.ds(pl.multiple_of((step * TIME_PAIRS + pair) * 128, 128), 128)
            q = x_ref[:, 0:16, lanes].reshape(ROWS, 128)
            k = x_ref[:, 16:32, lanes].reshape(ROWS, 128)
            v = x_ref[:, 32:48, lanes].reshape(ROWS, 128)
            total = None
            for head in range(2):
                mine = low if head == 0 else ~low
                scores = dot_nt(q, jnp.where(mine, k, zero)) * (1.0 / math.sqrt(HEAD))
                scores = jnp.where(keep, scores, -1e30)
                powers = jnp.exp(scores - jnp.max(scores, axis=-1, keepdims=True))
                weights = (powers * (1.0 / jnp.sum(powers, axis=-1, keepdims=True))).astype(BF16)
                part = dot(weights, jnp.where(mine, v, zero))
                total = part if total is None else total + part
            o_ref[:, :, lanes] = total.astype(BF16).reshape(FRAMES, 16, 128)
        return carry

    lax.fori_loop(0, BLOCKS // TIME_PAIRS, heads, 0)


def time_attention(lengths, qkv):
    return pl.pallas_call(
        time_kernel,
        in_specs=[
            pl.BlockSpec(memory_space=pltpu.SMEM),
            pl.BlockSpec(memory_space=pltpu.VMEM),
        ],
        out_shape=jax.ShapeDtypeStruct((FRAMES, 16, D), BF16),
        compiler_params=pltpu.CompilerParams(vmem_limit_bytes=16 << 20),
        name="time_attention",
    )(lengths, in_vmem(qkv))


def after_time_kernel(mixed_ref, patch_ref, w_ref, gain_ref, after_ref, normed_ref):
    after_time = patch_ref[...].astype(F32) + dot(mixed_ref[...], w_ref[...])
    after_ref[...] = after_time
    normed_ref[...] = norm_rows(after_time, gain_ref[...])


def after_time_step(mixed, patches, w_time, gain):
    return pl.pallas_call(
        after_time_kernel,
        out_shape=[
            jax.ShapeDtypeStruct((ROWS, D), F32),
            jax.ShapeDtypeStruct((ROWS, D), BF16),
        ],
        compiler_params=pltpu.CompilerParams(vmem_limit_bytes=24 << 20),
        name="after_time",
    )(mixed, patches, in_hbm(w_time), gain)


def spread_matrix():
    i = lax.broadcasted_iota(jnp.int32, (256, 192), 0)
    j = lax.broadcasted_iota(jnp.int32, (256, 192), 1)
    same = (i >> 5) == ((j & 15) >> 1)
    place = (i & 31) == 2 * (j >> 4) + (j & 1)
    return (same & place).astype(F32).astype(BF16)


def gather_matrix():
    j = lax.broadcasted_iota(jnp.int32, (192, 256), 0)
    i = lax.broadcasted_iota(jnp.int32, (192, 256), 1)
    same = (i >> 5) == ((j & 15) >> 1)
    place = (i & 31) == 2 * (j >> 4) + (j & 1)
    return (same & place).astype(F32).astype(BF16)


def unpack(block_ref, rows_ref, chunks):
    pick = gather_matrix()
    whole = chunks * 16
    for j in range(BLOCKS):
        rows_ref[0:whole, j * 128 : (j + 1) * 128] = block_ref[
            :, j * 16 : (j + 1) * 16, :
        ].reshape(whole, 128)
    for group in range(chunks // 8):
        packed = block_ref[group * 8 : (group + 1) * 8, 192:224, :].reshape(256, 128)
        last = dot(pick, packed).astype(BF16)
        at = whole + group * 16
        for j in range(BLOCKS):
            rows_ref[at : at + 16, j * 128 : (j + 1) * 128] = last[j * 16 : (j + 1) * 16, :]


GROUPS = 4
PAIRS = 2


def space_kernel(
    normed_ref,
    w_hbm,
    merge_hbm,
    after_ref,
    gain_ref,
    main_ref,
    last_ref,
    space_ref,
    send_ref,
    w_rows,
    merge,
    projected,
    spatial,
    sems,
):
    per_group = FRAMES // GROUPS
    high = per_group * 288

    def fetch(group, frame, z):
        f = group * per_group + frame
        return pltpu.make_async_copy(
            w_hbm.at[f, z],
            w_rows.at[pl.ds(f * 288, 288), pl.ds(z * 384, 384)],
            sems.at[group],
        )

    every = [(frame, z) for frame in range(per_group) for z in range(4)]
    for group in range(GROUPS):
        for frame, z in every:
            fetch(group, frame, z).start()
    fetch_merge = pltpu.make_async_copy(merge_hbm, merge, sems.at[GROUPS])
    fetch_merge.start()
    for group in range(GROUPS):
        for frame, z in every:
            fetch(group, frame, z).wait()
        rows = slice(group * high, (group + 1) * high)
        projected[:, rows] = dot_nt(normed_ref[...], w_rows[rows, :]).astype(BF16)

    low = lax.broadcasted_iota(jnp.int32, (ROWS, 128), 1) < HEAD
    zero = jnp.zeros((ROWS, 128), BF16)

    def heads(step, carry):
        for pair in range(PAIRS):
            first = pl.multiple_of((step * PAIRS + pair) * 128, 128)
            q = projected[:, pl.ds(first, 128)]
            k = projected[:, pl.ds(pl.multiple_of(first + D, 128), 128)]
            v = projected[:, pl.ds(pl.multiple_of(first + 2 * D, 128), 128)]
            mixed = None
            for head in range(2):
                mine = low if head == 0 else ~low
                scores = dot_nt(q, jnp.where(mine, k, zero)) * (1.0 / math.sqrt(HEAD))
                powers = jnp.exp(scores - jnp.max(scores, axis=-1, keepdims=True))
                weights = (powers * (1.0 / jnp.sum(powers, axis=-1, keepdims=True))).astype(BF16)
                part = dot(weights, jnp.where(mine, v, zero))
                mixed = part if mixed is None else mixed + part
            spatial[:, pl.ds(first, 128)] = mixed.astype(BF16)
        return carry

    lax.fori_loop(0, BLOCKS // PAIRS, heads, 0)
    fetch_merge.wait()
    after_space = after_ref[...] + dot(spatial[...], merge[...])
    space_ref[...] = after_space
    mixed_in = norm_rows(after_space, gain_ref[...])
    slot = lax.broadcasted_iota(jnp.int32, (512, ROWS), 0)
    chosen = (slot == main_ref[0:1, :]) | (slot == main_ref[1:2, :])
    rows = dot(chosen.astype(F32).astype(BF16), mixed_in).astype(BF16)
    slot = lax.broadcasted_iota(jnp.int32, (64, ROWS), 0)
    chosen = (slot == last_ref[0:1, :]) | (slot == last_ref[1:2, :])
    last = dot(chosen.astype(F32).astype(BF16), mixed_in).astype(BF16)
    for j in range(BLOCKS):
        piece = rows[:, j * 128 : (j + 1) * 128].reshape(EXPERTS, 16, 128)
        for copy in range(2):
            send_ref[:, copy, j * 16 : (j + 1) * 16, :] = piece
    spread = spread_matrix()
    for group in range(4):
        own = last[group * 16 : (group + 1) * 16, :]
        tall = jnp.concatenate([own[:, j * 128 : (j + 1) * 128] for j in range(BLOCKS)], axis=0)
        packed = dot(spread, tall).astype(BF16).reshape(8, 32, 128)
        for copy in range(2):
            send_ref[group * 8 : (group + 1) * 8, copy, 192:224, :] = packed


def space_step(normed, w_rows, w_merge, after_time, gain, main, last):
    whole = lambda i: (0, 0)
    anywhere = pl.BlockSpec(memory_space=pl.ANY)
    return pl.pallas_call(
        space_kernel,
        grid=(1,),
        in_specs=[
            pl.BlockSpec((ROWS, D), whole),
            anywhere,
            anywhere,
            pl.BlockSpec((ROWS, D), whole),
            pl.BlockSpec((1, D), whole),
            pl.BlockSpec((2, ROWS), whole),
            pl.BlockSpec((2, ROWS), whole),
        ],
        out_specs=[
            pl.BlockSpec((ROWS, D), whole),
            pl.BlockSpec((EXPERTS, 2, PACK, 128), lambda i: (0, 0, 0, 0)),
        ],
        out_shape=[
            jax.ShapeDtypeStruct((ROWS, D), F32),
            jax.ShapeDtypeStruct((EXPERTS, 2, PACK, 128), BF16),
        ],
        scratch_shapes=[
            pltpu.VMEM((3 * D, D), BF16),
            pltpu.VMEM((D, D), BF16),
            pltpu.VMEM((ROWS, 3 * D), BF16),
            pltpu.VMEM((ROWS, D), BF16),
            pltpu.SemaphoreType.DMA((GROUPS + 1,)),
        ],
        compiler_params=pltpu.CompilerParams(vmem_limit_bytes=VMEM),
        name="space_attention",
    )(normed, w_rows, in_hbm(w_merge), after_time, gain, main, last)


CHUNKS = 32
EXPERT_ROWS = CHUNKS * 18
CUT = 512
CUTS = D // CUT


def first_kernel(x_ref, expand_hbm, reduce_hbm, o_ref, expand, reduce, rows, hidden, sems):
    def fetch(n):
        cols = pl.ds((n % CUTS) * CUT, CUT)
        source, target = (expand_hbm, expand) if n < CUTS else (reduce_hbm, reduce)
        return pltpu.make_async_copy(source.at[:, :, cols], target.at[:, :, cols], sems.at[n])

    for n in range(2 * CUTS):
        fetch(n).start()
    expert_body(x_ref, expand, reduce, o_ref, rows, hidden, lambda n: fetch(n).wait())


def later_kernel(x_ref, expand, reduce, o_ref, rows, hidden):
    expert_body(x_ref, expand, reduce, o_ref, rows, hidden, lambda n: None)


def add_kernel(own_a, back_a, own_b, back_b, o_ref):
    step = pl.program_id(0)

    @pl.when(step < 2)
    def _():
        o_ref[...] = (own_a[...].astype(F32) + back_a[...].astype(F32)).astype(BF16)

    @pl.when(step >= 2)
    def _():
        o_ref[...] = (own_b[...].astype(F32) + back_b[...].astype(F32)).astype(BF16)


def add_parts(own_a, back_a, own_b, back_b):
    block = (CHUNKS // 2, PACK, 128)
    first = pl.BlockSpec(block, lambda i: (jnp.minimum(i, 1), 0, 0))
    second = pl.BlockSpec(block, lambda i: (jnp.maximum(i - 2, 0), 0, 0))
    return pl.pallas_call(
        add_kernel,
        grid=(4,),
        in_specs=[first, first, second, second],
        out_specs=pl.BlockSpec(block, lambda i: (i, 0, 0)),
        out_shape=pltpu.HBM((2 * CHUNKS, PACK, 128), BF16),
        compiler_params=pltpu.CompilerParams(vmem_limit_bytes=16 << 20),
        name="add_parts",
    )(own_a, back_a, own_b, back_b)


def expert_body(x_ref, expand, reduce, o_ref, rows, hidden, ready):
    whole = CHUNKS * 16
    unpack(x_ref, rows, CHUNKS)
    for n in range(CUTS):
        ready(n)
        inner = dot(rows[...], expand[0, :, n * CUT : (n + 1) * CUT])
        active = inner * (0.5 + 0.5 * lax.erf(inner * math.sqrt(0.5)))
        hidden[:, n * CUT : (n + 1) * CUT] = active.astype(BF16)
    spread = spread_matrix()
    tops = [[] for _ in range(CHUNKS // 8)]
    for n in range(CUTS):
        ready(CUTS + n)
        part = dot(hidden[...], reduce[0, :, n * CUT : (n + 1) * CUT])
        for j in range(CUT // 128):
            at = n * (CUT // 128) + j
            piece = part[:, j * 128 : (j + 1) * 128]
            main = piece[0:whole].reshape(CHUNKS, 16, 128)
            o_ref[:, at * 16 : (at + 1) * 16, :] = main.astype(BF16)
            for group in range(CHUNKS // 8):
                start = whole + group * 16
                tops[group].append(piece[start : start + 16].astype(BF16))
    for group in range(CHUNKS // 8):
        packed = dot(spread, jnp.concatenate(tops[group], axis=0)).reshape(8, 32, 128)
        at = group * 8
        o_ref[at : at + 8, 192:224, :] = packed.astype(BF16)


EXPERT_SCRATCH = [
    pltpu.VMEM((EXPERT_ROWS, D), BF16),
    pltpu.VMEM((EXPERT_ROWS, D), BF16),
]
EXPERT_COST = pl.CostEstimate(
    flops=EXPERT_ROWS * D * D * 4,
    bytes_accessed=2 * CHUNKS * PACK * 128 * 2,
    transcendentals=EXPERT_ROWS * D,
)
HALF = (CHUNKS, PACK, 128)


def first_experts(arrived, expand, reduce):
    anywhere = pl.BlockSpec(memory_space=pl.ANY)
    resident = pl.BlockSpec(memory_space=pltpu.VMEM)
    return pl.pallas_call(
        first_kernel,
        grid=(1,),
        in_specs=[pl.BlockSpec(HALF, lambda i: (0, 0, 0)), anywhere, anywhere],
        out_specs=[pl.BlockSpec(HALF, lambda i: (0, 0, 0)), resident, resident],
        out_shape=[
            jax.ShapeDtypeStruct(HALF, BF16),
            pltpu.VMEM((1, D, D), BF16),
            pltpu.VMEM((1, D, D), BF16),
        ],
        scratch_shapes=EXPERT_SCRATCH + [pltpu.SemaphoreType.DMA((2 * CUTS,))],
        compiler_params=pltpu.CompilerParams(vmem_limit_bytes=18 << 20),
        cost_estimate=EXPERT_COST,
        name="experts",
    )(arrived, in_hbm(expand), in_hbm(reduce))


def run_experts(half, arrived, expand, reduce):
    resident = pl.BlockSpec(memory_space=pltpu.VMEM)
    return pl.pallas_call(
        later_kernel,
        grid=(1,),
        in_specs=[pl.BlockSpec(HALF, lambda i: (half, 0, 0)), resident, resident],
        out_specs=pl.BlockSpec(HALF, lambda i: (0, 0, 0)),
        out_shape=jax.ShapeDtypeStruct(HALF, BF16),
        scratch_shapes=EXPERT_SCRATCH,
        compiler_params=pltpu.CompilerParams(vmem_limit_bytes=18 << 20),
        cost_estimate=EXPERT_COST,
        name="experts",
    )(arrived, in_vmem(expand), in_vmem(reduce))


def combine_kernel(x_ref, main_ref, last_ref, gate_ref, space_ref, o_ref, rows, totals):
    step = pl.program_id(0)

    @pl.when(step == 0)
    def _():
        totals[...] = jnp.zeros_like(totals)

    unpack(x_ref, rows, 16)
    at = lax.broadcasted_iota(jnp.int32, (ROWS, 288), 1)
    in_last = at >= 256
    expert = jnp.where(in_last, (at - 256) >> 2, at >> 5) + step * 8
    code = jnp.where(in_last, expert * 2 + (at & 1), expert * 16 + (at & 15))
    for k in range(2):
        wanted = jnp.where(in_last, last_ref[:, k : k + 1], main_ref[:, k : k + 1])
        totals[k] += dot((code == wanted).astype(F32).astype(BF16), rows[...])

    @pl.when(step == 3)
    def _():
        mix = totals[0] * gate_ref[:, 0:1] + totals[1] * gate_ref[:, 1:2]
        o_ref[...] = (space_ref[...] + mix).astype(BF16)


def combine(returned, main, last, gates, after_space):
    whole = lambda i: (0, 0)
    return pl.pallas_call(
        combine_kernel,
        grid=(4,),
        in_specs=[
            pl.BlockSpec((16, PACK, 128), lambda i: (i, 0, 0)),
            pl.BlockSpec((ROWS, 2), whole),
            pl.BlockSpec((ROWS, 2), whole),
            pl.BlockSpec((ROWS, 2), whole),
            pl.BlockSpec((ROWS, D), whole),
        ],
        out_specs=pl.BlockSpec((ROWS, D), whole),
        out_shape=jax.ShapeDtypeStruct((ROWS, D), BF16),
        scratch_shapes=[pltpu.VMEM((288, D), BF16), pltpu.VMEM((2, ROWS, D), F32)],
        compiler_params=pltpu.CompilerParams(vmem_limit_bytes=VMEM),
        name="combine",
    )(returned, main, last, gates, after_space)


def shards(
    patches,
    temporal_q,
    temporal_k,
    temporal_v,
    clip_lengths,
    w_time,
    gain_space,
    w_space,
    w_merge,
    gain_mix,
    expert_ids,
    gate_weights,
    w_expand,
    w_reduce,
):
    frame_axes, chip_axes = ("x", "y"), ("x", "y", "z")
    swap = [(0, 1), (1, 0)]

    own_rows = lax.dynamic_slice(
        w_space,
        (lax.axis_index("z") * 384, lax.axis_index("c") * 144),
        (384, 144),
    ).T
    w_rows = lax.all_gather(own_rows, ("x", "y", "z", "c"), axis=0, tiled=True)
    w_rows = w_rows.reshape(FRAMES, 4, 288, 384)

    qkv_own = jnp.concatenate(
        [a.reshape(FRAMES, 16, D) for a in (temporal_q, temporal_k, temporal_v)], axis=1
    )
    qkv = lax.all_to_all(qkv_own, frame_axes, split_axis=0, concat_axis=0, tiled=True)
    mixed = time_attention(clip_lengths, qkv)
    mixed = lax.all_to_all(mixed, frame_axes, split_axis=0, concat_axis=0, tiled=True)
    after_time, normed = after_time_step(
        mixed.reshape(ROWS, D), patches.reshape(ROWS, D), w_time, gain_space.reshape(1, D)
    )

    experts = expert_ids.reshape(ROWS * 2)
    index = jnp.arange(ROWS * 2, dtype=jnp.int32)
    earlier = (experts[:, None] == experts[None, :]) & (index[None, :] < index[:, None])
    slot = jnp.sum(earlier.astype(jnp.int32), axis=1)
    main = jnp.where(slot < MAIN, experts * MAIN + slot, -1).reshape(ROWS, 2)
    last = jnp.where(slot >= MAIN, experts * 2 + slot - MAIN, -1).reshape(ROWS, 2)

    after_space, outgoing = space_step(
        normed, w_rows, w_merge, after_time, gain_mix.reshape(1, D), main.T, last.T
    )
    arrived = lax.all_to_all(
        outgoing.reshape(64, PACK, 128), chip_axes, split_axis=0, concat_axis=0, tiled=True
    )
    theirs = lax.ppermute(arrived, "c", swap)
    part_own, expand, reduce = first_experts(arrived, w_expand, w_reduce)
    theirs, part_own = lax.optimization_barrier((theirs, part_own))
    part_a = run_experts(0, theirs, expand, reduce)
    back_a = lax.ppermute(part_a, "c", swap)
    part_b = run_experts(1, theirs, expand, reduce)
    back_b = lax.ppermute(part_b, "c", swap)
    part_own_b = run_experts(1, arrived, expand, reduce)
    sums = add_parts(part_own, back_a, part_own_b, back_b)
    returned = lax.all_to_all(sums, chip_axes, split_axis=0, concat_axis=0, tiled=True)
    out = combine(returned, main, last, gate_weights.reshape(ROWS, 2), after_space)
    return out.reshape(patches.shape)


def solution(mesh):
    grid = Mesh(mesh.devices.reshape(4, 4, 4, 2), ("x", "y", "z", "c"))
    frame, clip = ("x", "y"), ("z", "c")
    every = ("x", "y", "z", "c")
    return jax.shard_map(
        shards,
        mesh=grid,
        in_specs=(
            P(frame, clip, None, None),
            P(frame, clip, None, None),
            P(frame, clip, None, None),
            P(frame, clip, None, None),
            P(clip),
            P(),
            P(),
            P(None, frame),
            P(),
            P(),
            P(frame, clip, None, None),
            P(frame, clip, None, None),
            P(every, None, None),
            P(every, None, None),
        ),
        out_specs=P(frame, clip, None, None),
        check_vma=False,
    )
```

time: 350 us -> 287 us (0.82)
  Pallas kernels: 119 us -> 63.3 us
  local copies, waits for them, and re-layouts: 16.5 us -> 3.71 us
  waiting for transfers between devices: 113 us -> 119 us
    pallas_call x7 -> x8, Pallas kernels: 112 us -> 56.2 us  [the longest x3 18.5 us: run_experts(): pl.pallas_call(later_kernel, grid=(1,), in_specs=[pl.BlockSpec(HALF, lamb...]
    unnamed x34 -> x20, local copies, waits for them, and re-layouts: 14.8 us -> 2.59 us
    all_gather x1, waiting for transfers between devices: 18.4 us -> 26.5 us  [shards(): w_rows = lax.all_gather(own_rows, ('x', 'y', 'z', 'c'), axis=0, tiled=True)]
    ppermute x1, waiting for transfers between devices: 6.41 us -> 0.01 us  [shards(): theirs = lax.ppermute(arrived, 'c', swap)]
  transfers between devices with their start and end apart: 7 -> 7, of which waited for: 5 -> 4; matrix products, arithmetic and copies ran while one was open for 1% -> 1% of each run, Pallas kernels for 19% -> 9%
where the time goes in v2:
time: 287 us; the launch traced here: 282 us
  waiting for transfers between devices  119 us (41%)
  Pallas kernels  63.3 us (22%)
  blocking collectives  52.3 us (18%)
  starting transfers between devices  26.4 us (9%)
  between operations  14.2 us (5%)
  local copies, waits for them, and re-layouts  3.71 us (1%)
  other arithmetic  3.49 us (1%)
    all_to_all x1, blocking collectives, shards(): lax.all_to_all(outgoing.reshape(64, PACK, 128), chip_axes, split_axis=0,...  52.3 us
    all_to_all x1, waiting for transfers between devices, shards(): lax.all_to_all(sums, chip_axes, split_axis=0, concat_axis=0, tiled=True)  51.1 us
    all_to_all x1, waiting for transfers between devices, shards(): lax.all_to_all(qkv_own, frame_axes, split_axis=0, concat_axis=0, tiled=True)  29.8 us
    all_gather x1, waiting for transfers between devices, shards(): w_rows = lax.all_gather(own_rows, ('x', 'y', 'z', 'c'), axis=0, tiled=True)  26.5 us
    pallas_call x3, Pallas kernels, run_experts(): pl.pallas_call(later_kernel, grid=(1,), in_specs=[pl.BlockSpec(HALF, lamb...  18.5 us
    pallas_call x1, Pallas kernels, space_step(): pl.pallas_call(space_kernel, grid=(1,), in_specs=[pl.BlockSpec((ROWS, D),...  16.1 us
    all_to_all x1, waiting for transfers between devices, shards(): lax.all_to_all(mixed, frame_axes, split_axis=0, concat_axis=0, tiled=True)  11.2 us
    all_to_all x1, starting transfers between devices, shards(): lax.all_to_all(sums, chip_axes, split_axis=0, concat_axis=0, tiled=True)  10.4 us
  transfers between devices with their start and end apart: 7, of which 4 were waited for; matrix products, arithmetic and copies ran while one was open for 1% of the time, Pallas kernels for 9%

profile of v2, /device:TPU:82, one launch (start us, length us, event | category | flops | bytes accessed | tf_op | source)
XLA Modules:
  0.0 282.1 jit_solution(2218860449359964642)
XLA Ops:
  6.5 1.2 copy-done
  7.7 0.7 dynamic-slice_bitcast_fusion
  8.4 3.2 %pad_maximum_fusion = bf16[16,48,1536]{2,1,0:T(8,128)(2,1)} fusion(bf16[16,16,1536]{2,1,0:T(8,128)(2,1)} %bitcast.32, bf16[16,16,1536]{2,1,0:T(8,128)(2,1)} %bitcast.33, bf16[16,16,1536]{2,1,0:T(8,128)(2,1)} %bitcast.34), kind=kLoop, calls=%fused_computation | loop fusion | flops 7077888 | bytes 4718592 | tf_op jit(solution)/shard_map/concatenate | solution.py:452
  11.6 7.4 %all-to-all-start = ((bf16[16,48,1536]{2,1,0:T(8,128)(2,1)}), bf16[16,48,1536]{2,1,0:T(8,128)(2,1)S(1)}, u32[]{:S(2)}, u32[]{:S(2)}) async-start(bf16[16,48,1536]{2,1,0:T(8,128)(2,1)} %pad_maximum_fusion), calls=%async_computation | async-start | bytes 4718592 | tf_op jit(solution)/shard_map/all_to_all | solution.py:455
  19.6 29.8 %all-to-all-done.x_ref = bf16[16,48,1536]{2,1,0:T(8,128)(2,1)S(1)} async-done(((bf16[16,48,1536]{2,1,0:T(8,128)(2,1)}), bf16[16,48,1536]{2,1,0:T(8,128)(2,1)S(1)}, u32[]{:S(2)}, u32[]{:S(2)}) %all-to-all-start) | async-done | bytes 2359328 | tf_op jit(solution)/shard_map/all_to_all | solution.py:455
  49.4 6.2 %time_attention.1 = bf16[16,16,1536]{2,1,0:T(8,128)(2,1)} custom-call(s32[1]{0:T(128)S(6)} %copy.32.len_ref, bf16[16,48,1536]{2,1,0:T(8,128)(2,1)S(1)} %all-to-all-done.x_ref), custom_call_target="tpu_custom_call" | custom-call | tf_op jit(solution)/shard_map/time_attention/pallas_call | solution.py:78
  55.6 7.9 %all-to-all-start.1 = ((bf16[16,16,1536]{2,1,0:T(8,128)(2,1)}), bf16[16,16,1536]{2,1,0:T(8,128)(2,1)S(1)}, u32[]{:S(2)}, u32[]{:S(2)}) async-start(bf16[16,16,1536]{2,1,0:T(8,128)(2,1)} %time_attention.1), calls=%async_computation.1 | async-start | bytes 1572864 | tf_op jit(solution)/shard_map/all_to_all | solution.py:457
  63.9 0.3 convert_reduce_fusion
  64.1 0.1 reduce_sum.12
  64.5 11.2 %all-to-all-done.1 = bf16[16,16,1536]{2,1,0:T(8,128)(2,1)S(1)} async-done(((bf16[16,16,1536]{2,1,0:T(8,128)(2,1)}), bf16[16,16,1536]{2,1,0:T(8,128)(2,1)S(1)}, u32[]{:S(2)}, u32[]{:S(2)}) %all-to-all-start.1) | async-done | bytes 786464 | tf_op jit(solution)/shard_map/all_to_all | solution.py:457
  75.7 1.1 copy-done.4
  76.8 4.1 %after_time.1 = (f32[256,1536]{1,0:T(8,128)S(1)}, bf16[256,1536]{1,0:T(8,128)(2,1)S(1)}) custom-call(bf16[256,1536]{1,0:T(8,128)(2,1)S(1)} %bitcast.26, bf16[256,1536]{1,0:T(8,128)(2,1)S(1)} %bitcast.29, bf16[1536,1536]{1,0:T(8,128)(2,1)} %w_ref.1, f32[1,1536]{1,0:T(1,128)S(1)} %reshape.51.gain_ref), custom_call_target="tpu_custom_call" | custom-call | tf_op jit(solution)/shard_map/after_time/pallas_call | solution.py:97
  80.9 26.5 %all-gather.2.cloned.1.call-done = bf16[18432,384]{1,0:T(8,128)(2,1)} async-done(((bf16[144,384]{1,0:T(8,128)(2,1)}), bf16[18432,384]{1,0:T(8,128)(2,1)}) %all-gather.2.cloned.1.call-update) | async-done | bytes 14155792 | tf_op jit(solution)/shard_map/all_gather | solution.py:449
  107.4 16.1 %space_attention.1 = (f32[256,1536]{1,0:T(8,128)S(1)}, bf16[32,2,224,128]{3,2,1,0:T(8,128)(2,1)S(1)}) custom-call(bf16[256,1536]{1,0:T(8,128)(2,1)S(1)} %get-tuple-element.14.normed_ref, bf16[16,4,288,384]{3,2,1,0:T(8,128)(2,1)} %bitcast.31, bf16[1536,1536]{1,0:T(8,128)(2,1)} %merge_hbm.1, f32[256,1536]{1,0:T(8,128)S(1)} %get-tuple-element.15.after_ref, ...), custom_call_target="tpu_custom_call" | custom-call | tf_op jit(solution)/shard_map/space_attention/pallas_call | solution.py:229
  123.5 52.3 %all_to_all.20.x_ref = bf16[64,224,128]{2,1,0:T(8,128)(2,1)S(1)} all-to-all(bf16[64,224,128]{2,1,0:T(8,128)(2,1)S(1)} %bitcast.25), channel_id=1, replica_groups=mesh['x'=4,'y'=4,'z'=4,'c'=2] {'x','y','z'}, dimensions={0} | all-to-all | bytes 7340032 | tf_op jit(solution)/shard_map/all_to_all | solution.py:472
  175.9 8.7 %experts.4 = (bf16[32,224,128]{2,1,0:T(8,128)(2,1)S(1)}, bf16[1,1536,1536]{2,1,0:T(8,128)(2,1)S(1)}, bf16[1,1536,1536]{2,1,0:T(8,128)(2,1)S(1)}) custom-call(bf16[64,224,128]{2,1,0:T(8,128)(2,1)S(1)} %all_to_all.20.x_ref, bf16[1,1536,1536]{2,1,0:T(8,128)(2,1)} %expand_hbm.1, bf16[1,1536,1536]{2,1,0:T(8,128)(2,1)} %reduce_hbm.1), custom_call_target="tpu_custom_call" | custom-call | flops 5435817984 | bytes 3670016 | tf_op jit(solution)/shard_map/experts/pallas_call | solution.py:351
  184.6 6.1 %experts.7 = bf16[32,224,128]{2,1,0:T(8,128)(2,1)S(1)} custom-call(bf16[64,224,128]{2,1,0:T(8,128)(2,1)S(1)} %collective-permute-done.x_ref, bf16[1,1536,1536]{2,1,0:T(8,128)(2,1)S(1)} %get-tuple-element.20.expand, bf16[1,1536,1536]{2,1,0:T(8,128)(2,1)S(1)} %get-tuple-element.21.reduce), custom_call_target="tpu_custom_call" | custom-call | flops 5435817984 | bytes 3670016 | tf_op jit(solution)/shard_map/experts/pallas_call | solution.py:370
  190.7 6.3 %experts.5 = bf16[32,224,128]{2,1,0:T(8,128)(2,1)S(1)} custom-call(bf16[64,224,128]{2,1,0:T(8,128)(2,1)S(1)} %collective-permute-done.x_ref, bf16[1,1536,1536]{2,1,0:T(8,128)(2,1)S(1)} %get-tuple-element.20.expand, bf16[1,1536,1536]{2,1,0:T(8,128)(2,1)S(1)} %get-tuple-element.21.reduce), custom_call_target="tpu_custom_call" | custom-call | flops 5435817984 | bytes 3670016 | tf_op jit(solution)/shard_map/experts/pallas_call | solution.py:370
  197.0 0.6 collective-permute-start.1
  197.6 6.1 %experts.6.own_b = bf16[32,224,128]{2,1,0:T(8,128)(2,1)S(1)} custom-call(bf16[64,224,128]{2,1,0:T(8,128)(2,1)S(1)} %all_to_all.20.x_ref, bf16[1,1536,1536]{2,1,0:T(8,128)(2,1)S(1)} %get-tuple-element.20.expand, bf16[1,1536,1536]{2,1,0:T(8,128)(2,1)S(1)} %get-tuple-element.21.reduce), custom_call_target="tpu_custom_call" | custom-call | flops 5435817984 | bytes 3670016 | tf_op jit(solution)/shard_map/experts/pallas_call | solution.py:370
  203.7 2.7 add_parts.1
  206.4 10.4 %all-to-all-start.3 = ((bf16[64,224,128]{2,1,0:T(8,128)(2,1)}), bf16[64,224,128]{2,1,0:T(8,128)(2,1)}, u32[]{:S(2)}, u32[]{:S(2)}) async-start(bf16[64,224,128]{2,1,0:T(8,128)(2,1)} %add_parts.1), calls=%async_computation.3 | async-start | bytes 7340032 | tf_op jit(solution)/shard_map/all_to_all | solution.py:484
  217.0 51.1 %all-to-all-done.3.x_ref = bf16[64,224,128]{2,1,0:T(8,128)(2,1)} async-done(((bf16[64,224,128]{2,1,0:T(8,128)(2,1)}), bf16[64,224,128]{2,1,0:T(8,128)(2,1)}, u32[]{:S(2)}, u32[]{:S(2)}) %all-to-all-start.3) | async-done | bytes 3670048 | tf_op jit(solution)/shard_map/all_to_all | solution.py:484
  268.1 7.1 %combine.1 = bf16[256,1536]{1,0:T(8,128)(2,1)} custom-call(bf16[64,224,128]{2,1,0:T(8,128)(2,1)} %all-to-all-done.3.x_ref, s32[256,2]{1,0:T(8,128)S(1)} %get-tuple-element.24.main_ref, s32[256,2]{1,0:T(8,128)S(1)} %get-tuple-element.23.last_ref, f32[256,2]{1,0:T(8,128)S(1)} %bitcast.30, f32[256,1536]{1,0:T(8,128)S(1)} %copy-done.3), custom_call_target="tpu_custom_call" | custom-call | tf_op jit(solution)/shard_map/combine/pallas_call | solution.py:407
  (31 shorter events, 0.8 us)
Async XLA Ops:
  6.5 1.2 copy-start
  6.5 100.8 %all-gather.2.cloned.1.call-start = ((), (), s32[]{:S(2)}) async-start(), calls=%async_computation.4 | async-start | bytes 14266368 | tf_op jit(solution)/shard_map/all_gather | solution.py:449
  11.6 52.0 %copy-start.5 = (f32[1536]{0:T(1024)S(1)}, f32[1536]{0:T(1024)}, u32[]{:S(2)}) copy-start(f32[1536]{0:T(1024)} %param.20) | copy-start | bytes 18436
  11.6 52.0 %copy-start.6 = (f32[1536]{0:T(1024)S(1)}, f32[1536]{0:T(1024)}, u32[]{:S(2)}) copy-start(f32[1536]{0:T(1024)} %param.23) | copy-start | bytes 18436
  11.6 52.0 %copy-start.7 = (s32[1,1,256,2]{2,3,1,0:T(2,128)S(1)}, s32[1,1,256,2]{2,3,1,0:T(2,128)}, u32[]{:S(2)}) copy-start(s32[1,1,256,2]{2,3,1,0:T(2,128)} %param.24) | copy-start | bytes 6148
  11.6 37.8 %all-to-all-start = ((bf16[16,48,1536]{2,1,0:T(8,128)(2,1)}), bf16[16,48,1536]{2,1,0:T(8,128)(2,1)S(1)}, u32[]{:S(2)}, u32[]{:S(2)}) async-start(bf16[16,48,1536]{2,1,0:T(8,128)(2,1)} %pad_maximum_fusion), calls=%async_computation | async-start | bytes 4718592 | tf_op jit(solution)/shard_map/all_to_all | solution.py:455
  55.6 20.1 %all-to-all-start.1 = ((bf16[16,16,1536]{2,1,0:T(8,128)(2,1)}), bf16[16,16,1536]{2,1,0:T(8,128)(2,1)S(1)}, u32[]{:S(2)}, u32[]{:S(2)}) async-start(bf16[16,16,1536]{2,1,0:T(8,128)(2,1)} %time_attention.1), calls=%async_computation.1 | async-start | bytes 1572864 | tf_op jit(solution)/shard_map/all_to_all | solution.py:457
  75.7 1.1 copy-start.4
  123.5 52.3 %copy-start.2 = (f32[256,1536]{1,0:T(8,128)}, f32[256,1536]{1,0:T(8,128)S(1)}, u32[]{:S(2)}) copy-start(f32[256,1536]{1,0:T(8,128)S(1)} %get-tuple-element.22.space_ref) | copy-start | bytes 4718596
  175.9 8.7 %collective-permute-start = (bf16[64,224,128]{2,1,0:T(8,128)(2,1)S(1)}, bf16[64,224,128]{2,1,0:T(8,128)(2,1)S(1)}, u32[]{:S(2)}, u32[]{:S(2)}) collective-permute-start(bf16[64,224,128]{2,1,0:T(8,128)(2,1)S(1)} %all_to_all.20.x_ref), channel_id=1, source_target_pairs={{0,1},{1,0},{2,3},{3,2},{4,5},{5,4},{6,7},{7,6},{8,9},{9,8},{10,11... | collective-permute-start | bytes 11010056 | tf_op jit(solution)/shard_map/ppermute | solution.py:475
  197.0 6.8 %collective-permute-start.1 = (bf16[32,224,128]{2,1,0:T(8,128)(2,1)S(1)}, bf16[32,224,128]{2,1,0:T(8,128)(2,1)S(1)}, u32[]{:S(2)}, u32[]{:S(2)}) collective-permute-start(bf16[32,224,128]{2,1,0:T(8,128)(2,1)S(1)} %experts.5), channel_id=1, source_target_pairs={{0,1},{1,0},{2,3},{3,2},{4,5},{5,4},{6,7},{7,6},{8,9},{9,8},{10,11... | collective-permute-start | bytes 5505032 | tf_op jit(solution)/shard_map/ppermute | solution.py:479
  197.5 6.2 %collective-permute-start.2 = (bf16[32,224,128]{2,1,0:T(8,128)(2,1)S(1)}, bf16[32,224,128]{2,1,0:T(8,128)(2,1)S(1)}, u32[]{:S(2)}, u32[]{:S(2)}) collective-permute-start(bf16[32,224,128]{2,1,0:T(8,128)(2,1)S(1)} %experts.7), channel_id=1, source_target_pairs={{0,1},{1,0},{2,3},{3,2},{4,5},{5,4},{6,7},{7,6},{8,9},{9,8},{10,11... | collective-permute-start | bytes 5505032 | tf_op jit(solution)/shard_map/ppermute | solution.py:481
  206.4 10.5 %copy-start.8 = (f32[1,1,256,2]{2,3,1,0:T(2,128)S(1)}, f32[1,1,256,2]{2,3,1,0:T(2,128)}, u32[]{:S(2)}) copy-start(f32[1,1,256,2]{2,3,1,0:T(2,128)} %param.25) | copy-start | bytes 6148
  206.4 61.8 %copy-start.3 = (f32[256,1536]{1,0:T(8,128)S(1)}, f32[256,1536]{1,0:T(8,128)}, u32[]{:S(2)}) copy-start(f32[256,1536]{1,0:T(8,128)} %copy-done.2) | copy-start | bytes 4718596
  206.4 61.7 %all-to-all-start.3 = ((bf16[64,224,128]{2,1,0:T(8,128)(2,1)}), bf16[64,224,128]{2,1,0:T(8,128)(2,1)}, u32[]{:S(2)}, u32[]{:S(2)}) async-start(bf16[64,224,128]{2,1,0:T(8,128)(2,1)} %add_parts.1), calls=%async_computation.3 | async-start | bytes 7340032 | tf_op jit(solution)/shard_map/all_to_all | solution.py:484
  216.9 58.4 %copy-start.1 = (bf16[1536,288]{0,1:T(8,128)(2,1)S(1)}, bf16[1536,288]{0,1:T(8,128)(2,1)}, u32[]{:S(2)}) copy-start(bf16[1536,288]{0,1:T(8,128)(2,1)} %param.21) | copy-start | bytes 2654212
Sparse Core Ops, SparseCore 0:
  10.4 96.9 all-gather.1

commit v3 on v2

--- a/solution.py
+++ b/solution.py
@@ -1,4 +1,5 @@
 import math
+from functools import partial
 
 import jax
 import jax.numpy as jnp
@@ -38,6 +39,21 @@
     return pltpu.with_memory_space_constraint(array, pltpu.HBM)
 
 
+def attend_pair(q, k, v, keep=None):
+    low = lax.broadcasted_iota(jnp.int32, (ROWS, 128), 1) < HEAD
+    zero, one = jnp.zeros((ROWS, 128), BF16), jnp.ones((ROWS, 128), BF16)
+    parts = []
+    for mine in (low, ~low):
+        scores = dot_nt(q, jnp.where(mine, k, zero))
+        if keep is not None:
+            scores = jnp.where(keep, scores, -1e30)
+        top = jnp.max(scores, axis=-1, keepdims=True)
+        powers = jnp.exp2((scores - top) * (1.0 / (math.sqrt(HEAD) * math.log(2.0))))
+        parts.append(dot(powers.astype(BF16), jnp.where(mine, v, one)))
+    sums = pltpu.roll(jnp.where(low, parts[1], parts[0]), HEAD, 1)
+    return (jnp.where(low, parts[0], parts[1]) / sums).astype(BF16)
+
+
 def norm_rows(values, gain):
     centre = values - jnp.mean(values, axis=-1, keepdims=True)
     spread = jnp.mean(centre * centre, axis=-1, keepdims=True)
@@ -51,24 +67,14 @@
     row = lax.broadcasted_iota(jnp.int32, (ROWS, ROWS), 0)
     col = lax.broadcasted_iota(jnp.int32, (ROWS, ROWS), 1)
     keep = ((row & 15) == (col & 15)) & ((col >> 4) < len_ref[0])
-    low = lax.broadcasted_iota(jnp.int32, (ROWS, 128), 1) < HEAD
-    zero = jnp.zeros((ROWS, 128), BF16)
+
     def heads(step, carry):
         for pair in range(TIME_PAIRS):
             lanes = pl.ds(pl.multiple_of((step * TIME_PAIRS + pair) * 128, 128), 128)
             q = x_ref[:, 0:16, lanes].reshape(ROWS, 128)
             k = x_ref[:, 16:32, lanes].reshape(ROWS, 128)
             v = x_ref[:, 32:48, lanes].reshape(ROWS, 128)
-            total = None
-            for head in range(2):
-                mine = low if head == 0 else ~low
-                scores = dot_nt(q, jnp.where(mine, k, zero)) * (1.0 / math.sqrt(HEAD))
-                scores = jnp.where(keep, scores, -1e30)
-                powers = jnp.exp(scores - jnp.max(scores, axis=-1, keepdims=True))
-                weights = (powers * (1.0 / jnp.sum(powers, axis=-1, keepdims=True))).astype(BF16)
-                part = dot(weights, jnp.where(mine, v, zero))
-                total = part if total is None else total + part
-            o_ref[:, :, lanes] = total.astype(BF16).reshape(FRAMES, 16, 128)
+            o_ref[:, :, lanes] = attend_pair(q, k, v, keep).reshape(FRAMES, 16, 128)
         return carry
 
     lax.fori_loop(0, BLOCKS // TIME_PAIRS, heads, 0)
@@ -136,8 +142,8 @@
             rows_ref[at : at + 16, j * 128 : (j + 1) * 128] = last[j * 16 : (j + 1) * 16, :]
 
 
-GROUPS = 4
-PAIRS = 2
+GROUPS = ((0, 1, 5, 6, 10, 11), (2, 7, 12, 13), (3, 8, 9, 14), (4, 15))
+QUARTER = D // len(GROUPS)
 
 
 def space_kernel(
@@ -152,54 +158,36 @@
     send_ref,
     w_rows,
     merge,
-    projected,
     spatial,
     sems,
 ):
-    per_group = FRAMES // GROUPS
-    high = per_group * 288
-
     def fetch(group, frame, z):
-        f = group * per_group + frame
         return pltpu.make_async_copy(
-            w_hbm.at[f, z],
-            w_rows.at[pl.ds(f * 288, 288), pl.ds(z * 384, 384)],
+            w_hbm.at[frame, z],
+            w_rows.at[pl.ds(frame * 288, 288), pl.ds(z * 384, 384)],
             sems.at[group],
         )
 
-    every = [(frame, z) for frame in range(per_group) for z in range(4)]
-    for group in range(GROUPS):
-        for frame, z in every:
-            fetch(group, frame, z).start()
-    fetch_merge = pltpu.make_async_copy(merge_hbm, merge, sems.at[GROUPS])
+    pieces = [[(frame, z) for frame in frames for z in range(4)] for frames in GROUPS]
+    for group in range(len(GROUPS)):
+        for count, (frame, z) in enumerate(pieces[group]):
+            fetch(group, frame, z).start(priority=count % 2)
+    fetch_merge = pltpu.make_async_copy(merge_hbm, merge, sems.at[len(GROUPS)])
     fetch_merge.start()
-    for group in range(GROUPS):
-        for frame, z in every:
+    for group in range(len(GROUPS)):
+        for frame, z in pieces[group]:
             fetch(group, frame, z).wait()
-        rows = slice(group * high, (group + 1) * high)
-        projected[:, rows] = dot_nt(normed_ref[...], w_rows[rows, :]).astype(BF16)
-
-    low = lax.broadcasted_iota(jnp.int32, (ROWS, 128), 1) < HEAD
-    zero = jnp.zeros((ROWS, 128), BF16)
-
-    def heads(step, carry):
-        for pair in range(PAIRS):
-            first = pl.multiple_of((step * PAIRS + pair) * 128, 128)
-            q = projected[:, pl.ds(first, 128)]
-            k = projected[:, pl.ds(pl.multiple_of(first + D, 128), 128)]
-            v = projected[:, pl.ds(pl.multiple_of(first + 2 * D, 128), 128)]
-            mixed = None
-            for head in range(2):
-                mine = low if head == 0 else ~low
-                scores = dot_nt(q, jnp.where(mine, k, zero)) * (1.0 / math.sqrt(HEAD))
-                powers = jnp.exp(scores - jnp.max(scores, axis=-1, keepdims=True))
-                weights = (powers * (1.0 / jnp.sum(powers, axis=-1, keepdims=True))).astype(BF16)
-                part = dot(weights, jnp.where(mine, v, zero))
-                mixed = part if mixed is None else mixed + part
-            spatial[:, pl.ds(first, 128)] = mixed.astype(BF16)
-        return carry
-
-    lax.fori_loop(0, BLOCKS // PAIRS, heads, 0)
+        q_all, k_all, v_all = (
+            dot_nt(
+                normed_ref[...], w_rows[part * D + group * QUARTER : part * D + (group + 1) * QUARTER]
+            ).astype(BF16)
+            for part in range(3)
+        )
+        for pair in range(QUARTER // 128):
+            lanes = slice(pair * 128, (pair + 1) * 128)
+            q, k, v = q_all[:, lanes], k_all[:, lanes], v_all[:, lanes]
+            at = group * QUARTER + pair * 128
+            spatial[:, at : at + 128] = attend_pair(q, k, v)
     fetch_merge.wait()
     after_space = after_ref[...] + dot(spatial[...], merge[...])
     space_ref[...] = after_space
@@ -224,38 +212,30 @@
 
 
 def space_step(normed, w_rows, w_merge, after_time, gain, main, last):
-    whole = lambda i: (0, 0)
+    resident = pl.BlockSpec(memory_space=pltpu.VMEM)
     anywhere = pl.BlockSpec(memory_space=pl.ANY)
     return pl.pallas_call(
         space_kernel,
-        grid=(1,),
-        in_specs=[
-            pl.BlockSpec((ROWS, D), whole),
-            anywhere,
-            anywhere,
-            pl.BlockSpec((ROWS, D), whole),
-            pl.BlockSpec((1, D), whole),
-            pl.BlockSpec((2, ROWS), whole),
-            pl.BlockSpec((2, ROWS), whole),
-        ],
-        out_specs=[
-            pl.BlockSpec((ROWS, D), whole),
-            pl.BlockSpec((EXPERTS, 2, PACK, 128), lambda i: (0, 0, 0, 0)),
-        ],
+        in_specs=[resident, anywhere, anywhere] + [resident] * 4,
+        out_specs=[resident] * 2,
         out_shape=[
-            jax.ShapeDtypeStruct((ROWS, D), F32),
-            jax.ShapeDtypeStruct((EXPERTS, 2, PACK, 128), BF16),
+            pltpu.VMEM((ROWS, D), F32),
+            pltpu.VMEM((EXPERTS, 2, PACK, 128), BF16),
         ],
         scratch_shapes=[
             pltpu.VMEM((3 * D, D), BF16),
             pltpu.VMEM((D, D), BF16),
-            pltpu.VMEM((ROWS, 3 * D), BF16),
             pltpu.VMEM((ROWS, D), BF16),
-            pltpu.SemaphoreType.DMA((GROUPS + 1,)),
-        ],
-        compiler_params=pltpu.CompilerParams(vmem_limit_bytes=VMEM),
+            pltpu.SemaphoreType.DMA((len(GROUPS) + 1,)),
+        ],
+        compiler_params=pltpu.CompilerParams(vmem_limit_bytes=32 << 20),
         name="space_attention",
-    )(normed, w_rows, in_hbm(w_merge), after_time, gain, main, last)
+    )(
+        in_vmem(normed),
+        in_hbm(w_rows),
+        in_hbm(w_merge),
+        *(in_vmem(a) for a in (after_time, gain, main, last)),
+    )
 
 
 CHUNKS = 32
@@ -264,7 +244,7 @@
 CUTS = D // CUT
 
 
-def first_kernel(x_ref, expand_hbm, reduce_hbm, o_ref, expand, reduce, rows, hidden, sems):
+def first_kernel(half, x_ref, expand_hbm, reduce_hbm, o_ref, expand, reduce, rows, hidden, sems):
     def fetch(n):
         cols = pl.ds((n % CUTS) * CUT, CUT)
         source, target = (expand_hbm, expand) if n < CUTS else (reduce_hbm, reduce)
@@ -272,11 +252,11 @@
 
     for n in range(2 * CUTS):
         fetch(n).start()
-    expert_body(x_ref, expand, reduce, o_ref, rows, hidden, lambda n: fetch(n).wait())
-
-
-def later_kernel(x_ref, expand, reduce, o_ref, rows, hidden):
-    expert_body(x_ref, expand, reduce, o_ref, rows, hidden, lambda n: None)
+    expert_body(half, x_ref, expand, reduce, o_ref, rows, hidden, lambda n: fetch(n).wait())
+
+
+def later_kernel(half, x_ref, expand, reduce, o_ref, rows, hidden):
+    expert_body(half, x_ref, expand, reduce, o_ref, rows, hidden, lambda n: None)
 
 
 def add_kernel(own_a, back_a, own_b, back_b, o_ref):
@@ -306,9 +286,9 @@
     )(own_a, back_a, own_b, back_b)
 
 
-def expert_body(x_ref, expand, reduce, o_ref, rows, hidden, ready):
+def expert_body(half, x_ref, expand, reduce, o_ref, rows, hidden, ready):
     whole = CHUNKS * 16
-    unpack(x_ref, rows, CHUNKS)
+    unpack(x_ref.at[half * CHUNKS : (half + 1) * CHUNKS], rows, CHUNKS)
     for n in range(CUTS):
         ready(n)
         inner = dot(rows[...], expand[0, :, n * CUT : (n + 1) * CUT])
@@ -345,81 +325,79 @@
 HALF = (CHUNKS, PACK, 128)
 
 
+RESIDENT = pl.BlockSpec(memory_space=pltpu.VMEM)
+
+
 def first_experts(arrived, expand, reduce):
     anywhere = pl.BlockSpec(memory_space=pl.ANY)
-    resident = pl.BlockSpec(memory_space=pltpu.VMEM)
-    return pl.pallas_call(
-        first_kernel,
-        grid=(1,),
-        in_specs=[pl.BlockSpec(HALF, lambda i: (0, 0, 0)), anywhere, anywhere],
-        out_specs=[pl.BlockSpec(HALF, lambda i: (0, 0, 0)), resident, resident],
+    return pl.pallas_call(
+        partial(first_kernel, 0),
+        in_specs=[RESIDENT, anywhere, anywhere],
+        out_specs=[RESIDENT] * 3,
         out_shape=[
-            jax.ShapeDtypeStruct(HALF, BF16),
+            pltpu.VMEM(HALF, BF16),
             pltpu.VMEM((1, D, D), BF16),
             pltpu.VMEM((1, D, D), BF16),
         ],
         scratch_shapes=EXPERT_SCRATCH + [pltpu.SemaphoreType.DMA((2 * CUTS,))],
-        compiler_params=pltpu.CompilerParams(vmem_limit_bytes=18 << 20),
+        compiler_params=pltpu.CompilerParams(vmem_limit_bytes=16 << 20),
         cost_estimate=EXPERT_COST,
         name="experts",
-    )(arrived, in_hbm(expand), in_hbm(reduce))
+    )(in_vmem(arrived), in_hbm(expand), in_hbm(reduce))
 
 
 def run_experts(half, arrived, expand, reduce):
-    resident = pl.BlockSpec(memory_space=pltpu.VMEM)
-    return pl.pallas_call(
-        later_kernel,
-        grid=(1,),
-        in_specs=[pl.BlockSpec(HALF, lambda i: (half, 0, 0)), resident, resident],
-        out_specs=pl.BlockSpec(HALF, lambda i: (0, 0, 0)),
-        out_shape=jax.ShapeDtypeStruct(HALF, BF16),
+    return pl.pallas_call(
+        partial(later_kernel, half),
+        in_specs=[RESIDENT] * 3,
+        out_specs=RESIDENT,
+        out_shape=pltpu.VMEM(HALF, BF16),
         scratch_shapes=EXPERT_SCRATCH,
-        compiler_params=pltpu.CompilerParams(vmem_limit_bytes=18 << 20),
+        compiler_params=pltpu.CompilerParams(vmem_limit_bytes=16 << 20),
         cost_estimate=EXPERT_COST,
         name="experts",
-    )(arrived, in_vmem(expand), in_vmem(reduce))
-
-
-def combine_kernel(x_ref, main_ref, last_ref, gate_ref, space_ref, o_ref, rows, totals):
-    step = pl.program_id(0)
-
-    @pl.when(step == 0)
-    def _():
-        totals[...] = jnp.zeros_like(totals)
-
-    unpack(x_ref, rows, 16)
-    at = lax.broadcasted_iota(jnp.int32, (ROWS, 288), 1)
-    in_last = at >= 256
-    expert = jnp.where(in_last, (at - 256) >> 2, at >> 5) + step * 8
-    code = jnp.where(in_last, expert * 2 + (at & 1), expert * 16 + (at & 15))
-    for k in range(2):
-        wanted = jnp.where(in_last, last_ref[:, k : k + 1], main_ref[:, k : k + 1])
-        totals[k] += dot((code == wanted).astype(F32).astype(BF16), rows[...])
-
-    @pl.when(step == 3)
-    def _():
-        mix = totals[0] * gate_ref[:, 0:1] + totals[1] * gate_ref[:, 1:2]
-        o_ref[...] = (space_ref[...] + mix).astype(BF16)
+    )(in_vmem(arrived), in_vmem(expand), in_vmem(reduce))
+
+
+def combine_kernel(x_hbm, main_ref, last_ref, gate_ref, space_ref, o_ref, chunks, rows, sems):
+    def fetch(part):
+        at = pl.ds(part * CHUNKS, CHUNKS)
+        return pltpu.make_async_copy(x_hbm.at[at], chunks.at[at], sems.at[part])
+
+    for part in range(2):
+        fetch(part).start()
+    at = lax.broadcasted_iota(jnp.int32, (2 * ROWS, EXPERT_ROWS), 1)
+    in_last = at >= CHUNKS * MAIN
+    last_code = ((at - CHUNKS * MAIN) >> 2) * 2 + (at & 1)
+    main_code = (at >> 5) * MAIN + (at & 15)
+    code = jnp.where(in_last, last_code, main_code)
+    wanted = jnp.where(in_last, last_ref[...], main_ref[...])
+    step = jnp.where(in_last, CHUNKS, CHUNKS // 2 * MAIN)
+    picked = None
+    for part in range(2):
+        fetch(part).wait()
+        half = rows.at[part * EXPERT_ROWS : (part + 1) * EXPERT_ROWS]
+        unpack(chunks.at[part * CHUNKS : (part + 1) * CHUNKS], half, CHUNKS)
+        chosen = (code + part * step == wanted).astype(F32).astype(BF16)
+        term = dot(chosen, half[...])
+        picked = term if picked is None else picked + term
+    mix = picked[0:ROWS] * gate_ref[:, 0:1] + picked[ROWS:] * gate_ref[:, 1:2]
+    o_ref[...] = (space_ref[...] + mix).astype(BF16)
 
 
 def combine(returned, main, last, gates, after_space):
-    whole = lambda i: (0, 0)
     return pl.pallas_call(
         combine_kernel,
-        grid=(4,),
-        in_specs=[
-            pl.BlockSpec((16, PACK, 128), lambda i: (i, 0, 0)),
-            pl.BlockSpec((ROWS, 2), whole),
-            pl.BlockSpec((ROWS, 2), whole),
-            pl.BlockSpec((ROWS, 2), whole),
-            pl.BlockSpec((ROWS, D), whole),
-        ],
-        out_specs=pl.BlockSpec((ROWS, D), whole),
+        in_specs=[pl.BlockSpec(memory_space=pl.ANY)] + [pl.BlockSpec(memory_space=pltpu.VMEM)] * 4,
         out_shape=jax.ShapeDtypeStruct((ROWS, D), BF16),
-        scratch_shapes=[pltpu.VMEM((288, D), BF16), pltpu.VMEM((2, ROWS, D), F32)],
+        scratch_shapes=[
+            pltpu.VMEM((2 * CHUNKS, PACK, 128), BF16),
+            pltpu.VMEM((2 * EXPERT_ROWS, D), BF16),
+            pltpu.SemaphoreType.DMA((2,)),
+        ],
         compiler_params=pltpu.CompilerParams(vmem_limit_bytes=VMEM),
         name="combine",
-    )(returned, main, last, gates, after_space)
+    )(in_hbm(returned), *map(in_vmem, (main, last, gates, after_space)))
 
 
 def shards(
@@ -482,6 +460,7 @@
     part_own_b = run_experts(1, arrived, expand, reduce)
     sums = add_parts(part_own, back_a, part_own_b, back_b)
     returned = lax.all_to_all(sums, chip_axes, split_axis=0, concat_axis=0, tiled=True)
+    main, last = (codes.T.reshape(2 * ROWS, 1) for codes in (main, last))
     out = combine(returned, main, last, gate_weights.reshape(ROWS, 2), after_space)
     return out.reshape(patches.shape)
 

time: 287 us -> 286 us (level)
  transfers between devices with their start and end apart: 7 -> 7, of which waited for: 4 -> 4; matrix products, arithmetic and copies ran while one was open for 1% -> 2% of each run, Pallas kernels for 9% -> 9%
where the time goes in v3:
time: 286 us; the launch traced here: 282 us
  waiting for transfers between devices  119 us (42%)
  Pallas kernels  61.3 us (21%)
  blocking collectives  52.3 us (18%)
  starting transfers between devices  26.4 us (9%)
  between operations  14.3 us (5%)
  local copies, waits for them, and re-layouts  5.15 us (2%)
  other arithmetic  3.46 us (1%)
    all_to_all x1, blocking collectives, shards(): lax.all_to_all(outgoing.reshape(64, PACK, 128), chip_axes, split_axis=0,...  52.3 us
    all_to_all x1, waiting for transfers between devices, shards(): lax.all_to_all(sums, chip_axes, split_axis=0, concat_axis=0, tiled=True)  50.6 us
    all_to_all x1, waiting for transfers between devices, shards(): lax.all_to_all(qkv_own, frame_axes, split_axis=0, concat_axis=0, tiled=True)  29.8 us
    all_gather x1, waiting for transfers between devices, shards(): w_rows = lax.all_gather(own_rows, ('x', 'y', 'z', 'c'), axis=0, tiled=True)  27.1 us
    pallas_call x3, Pallas kernels, run_experts(): pl.pallas_call(partial(later_kernel, half), in_specs=[RESIDENT] * 3, out_...  18.5 us
    pallas_call x1, Pallas kernels, space_step(): pl.pallas_call(space_kernel, in_specs=[resident, anywhere, anywhere] + [r...  16.4 us
    all_to_all x1, waiting for transfers between devices, shards(): lax.all_to_all(mixed, frame_axes, split_axis=0, concat_axis=0, tiled=True)  11.3 us
    all_to_all x1, starting transfers between devices, shards(): lax.all_to_all(sums, chip_axes, split_axis=0, concat_axis=0, tiled=True)  10.4 us
  transfers between devices with their start and end apart: 7, of which 4 were waited for; matrix products, arithmetic and copies ran while one was open for 2% of the time, Pallas kernels for 9%

profile of v3, /device:TPU:82, one launch (start us, length us, event | category | flops | bytes accessed | tf_op | source)
XLA Modules:
  0.0 281.8 jit_solution(17023242054920257971)
XLA Ops:
  6.5 1.2 copy-done
  7.7 0.7 dynamic-slice_bitcast_fusion
  8.4 3.2 %pad_maximum_fusion = bf16[16,48,1536]{2,1,0:T(8,128)(2,1)} fusion(bf16[16,16,1536]{2,1,0:T(8,128)(2,1)} %bitcast.52, bf16[16,16,1536]{2,1,0:T(8,128)(2,1)} %bitcast.53, bf16[16,16,1536]{2,1,0:T(8,128)(2,1)} %bitcast.54), kind=kLoop, calls=%fused_computation | loop fusion | flops 7077888 | bytes 4718592 | tf_op jit(solution)/shard_map/concatenate | solution.py:430
  11.6 7.4 %all-to-all-start = ((bf16[16,48,1536]{2,1,0:T(8,128)(2,1)}), bf16[16,48,1536]{2,1,0:T(8,128)(2,1)S(1)}, u32[]{:S(2)}, u32[]{:S(2)}) async-start(bf16[16,48,1536]{2,1,0:T(8,128)(2,1)} %pad_maximum_fusion), calls=%async_computation | async-start | bytes 4718592 | tf_op jit(solution)/shard_map/all_to_all | solution.py:433
  19.6 29.8 %all-to-all-done.x_ref = bf16[16,48,1536]{2,1,0:T(8,128)(2,1)S(1)} async-done(((bf16[16,48,1536]{2,1,0:T(8,128)(2,1)}), bf16[16,48,1536]{2,1,0:T(8,128)(2,1)S(1)}, u32[]{:S(2)}, u32[]{:S(2)}) %all-to-all-start) | async-done | bytes 2359328 | tf_op jit(solution)/shard_map/all_to_all | solution.py:433
  49.4 5.2 %time_attention.1 = bf16[16,16,1536]{2,1,0:T(8,128)(2,1)} custom-call(s32[1]{0:T(128)S(6)} %copy.36.len_ref, bf16[16,48,1536]{2,1,0:T(8,128)(2,1)S(1)} %all-to-all-done.x_ref), custom_call_target="tpu_custom_call" | custom-call | tf_op jit(solution)/shard_map/time_attention/pallas_call | solution.py:84
  54.6 7.9 %all-to-all-start.1 = ((bf16[16,16,1536]{2,1,0:T(8,128)(2,1)}), bf16[16,16,1536]{2,1,0:T(8,128)(2,1)S(1)}, u32[]{:S(2)}, u32[]{:S(2)}) async-start(bf16[16,16,1536]{2,1,0:T(8,128)(2,1)} %time_attention.1), calls=%async_computation.1 | async-start | bytes 1572864 | tf_op jit(solution)/shard_map/all_to_all | solution.py:435
  62.9 0.3 convert_reduce_fusion
  63.4 11.3 %all-to-all-done.1 = bf16[16,16,1536]{2,1,0:T(8,128)(2,1)S(1)} async-done(((bf16[16,16,1536]{2,1,0:T(8,128)(2,1)}), bf16[16,16,1536]{2,1,0:T(8,128)(2,1)S(1)}, u32[]{:S(2)}, u32[]{:S(2)}) %all-to-all-start.1) | async-done | bytes 786464 | tf_op jit(solution)/shard_map/all_to_all | solution.py:435
  74.7 1.1 copy-done.4
  75.9 4.1 %after_time.1 = (f32[256,1536]{1,0:T(8,128)S(1)}, bf16[256,1536]{1,0:T(8,128)(2,1)S(1)}) custom-call(bf16[256,1536]{1,0:T(8,128)(2,1)S(1)} %bitcast.46, bf16[256,1536]{1,0:T(8,128)(2,1)S(1)} %bitcast.49, bf16[1536,1536]{1,0:T(8,128)(2,1)} %w_ref.1, f32[1,1536]{1,0:T(1,128)S(1)} %reshape.57.gain_ref), custom_call_target="tpu_custom_call" | custom-call | tf_op jit(solution)/shard_map/after_time/pallas_call | solution.py:103
  79.9 27.1 %all-gather.2.cloned.1.call-done = bf16[18432,384]{1,0:T(8,128)(2,1)} async-done(((bf16[144,384]{1,0:T(8,128)(2,1)}), bf16[18432,384]{1,0:T(8,128)(2,1)}) %all-gather.2.cloned.1.call-update) | async-done | bytes 14155792 | tf_op jit(solution)/shard_map/all_gather | solution.py:427
  107.0 16.4 %space_attention.1 = (f32[256,1536]{1,0:T(8,128)S(1)}, bf16[32,2,224,128]{3,2,1,0:T(8,128)(2,1)S(1)}) custom-call(bf16[256,1536]{1,0:T(8,128)(2,1)S(1)} %get-tuple-element.14.normed_ref, bf16[16,4,288,384]{3,2,1,0:T(8,128)(2,1)} %bitcast.51, bf16[1536,1536]{1,0:T(8,128)(2,1)} %merge_hbm.1, f32[256,1536]{1,0:T(8,128)S(1)} %get-tuple-element.15.after_ref, ...), custom_call_target="tpu_custom_call" | custom-call | tf_op jit(solution)/shard_map/space_attention/pallas_call | solution.py:217
  123.4 1.2 copy-done.2
  124.7 52.3 %all_to_all.20.x_ref = bf16[64,224,128]{2,1,0:T(8,128)(2,1)S(1)} all-to-all(bf16[64,224,128]{2,1,0:T(8,128)(2,1)S(1)} %bitcast.45), channel_id=1, replica_groups=mesh['x'=4,'y'=4,'z'=4,'c'=2] {'x','y','z'}, dimensions={0} | all-to-all | bytes 7340032 | tf_op jit(solution)/shard_map/all_to_all | solution.py:450
  177.0 8.7 %experts.4 = (bf16[32,224,128]{2,1,0:T(8,128)(2,1)S(1)}, bf16[1,1536,1536]{2,1,0:T(8,128)(2,1)S(1)}, bf16[1,1536,1536]{2,1,0:T(8,128)(2,1)S(1)}) custom-call(bf16[64,224,128]{2,1,0:T(8,128)(2,1)S(1)} %all_to_all.20.x_ref, bf16[1,1536,1536]{2,1,0:T(8,128)(2,1)} %expand_hbm.1, bf16[1,1536,1536]{2,1,0:T(8,128)(2,1)} %reduce_hbm.1), custom_call_target="tpu_custom_call" | custom-call | flops 5435817984 | bytes 3670016 | tf_op jit(solution)/shard_map/experts/pallas_call | solution.py:333
  185.7 6.1 %experts.7 = bf16[32,224,128]{2,1,0:T(8,128)(2,1)S(1)} custom-call(bf16[64,224,128]{2,1,0:T(8,128)(2,1)S(1)} %collective-permute-done.x_ref, bf16[1,1536,1536]{2,1,0:T(8,128)(2,1)S(1)} %get-tuple-element.20.expand, bf16[1,1536,1536]{2,1,0:T(8,128)(2,1)S(1)} %get-tuple-element.21.reduce), custom_call_target="tpu_custom_call" | custom-call | flops 5435817984 | bytes 3670016 | tf_op jit(solution)/shard_map/experts/pallas_call | solution.py:350
  191.8 6.3 %experts.5 = bf16[32,224,128]{2,1,0:T(8,128)(2,1)S(1)} custom-call(bf16[64,224,128]{2,1,0:T(8,128)(2,1)S(1)} %collective-permute-done.x_ref, bf16[1,1536,1536]{2,1,0:T(8,128)(2,1)S(1)} %get-tuple-element.20.expand, bf16[1,1536,1536]{2,1,0:T(8,128)(2,1)S(1)} %get-tuple-element.21.reduce), custom_call_target="tpu_custom_call" | custom-call | flops 5435817984 | bytes 3670016 | tf_op jit(solution)/shard_map/experts/pallas_call | solution.py:350
  198.1 0.6 collective-permute-start.1
  198.8 6.1 %experts.6.own_b = bf16[32,224,128]{2,1,0:T(8,128)(2,1)S(1)} custom-call(bf16[64,224,128]{2,1,0:T(8,128)(2,1)S(1)} %all_to_all.20.x_ref, bf16[1,1536,1536]{2,1,0:T(8,128)(2,1)S(1)} %get-tuple-element.20.expand, bf16[1,1536,1536]{2,1,0:T(8,128)(2,1)S(1)} %get-tuple-element.21.reduce), custom_call_target="tpu_custom_call" | custom-call | flops 5435817984 | bytes 3670016 | tf_op jit(solution)/shard_map/experts/pallas_call | solution.py:350
  204.9 2.7 add_parts.1
  207.5 10.4 %all-to-all-start.3 = ((bf16[64,224,128]{2,1,0:T(8,128)(2,1)}), bf16[64,224,128]{2,1,0:T(8,128)(2,1)}, u32[]{:S(2)}, u32[]{:S(2)}) async-start(bf16[64,224,128]{2,1,0:T(8,128)(2,1)} %add_parts.1), calls=%async_computation.3 | async-start | bytes 7340032 | tf_op jit(solution)/shard_map/all_to_all | solution.py:462
  218.5 50.6 %all-to-all-done.3.x_hbm = bf16[64,224,128]{2,1,0:T(8,128)(2,1)} async-done(((bf16[64,224,128]{2,1,0:T(8,128)(2,1)}), bf16[64,224,128]{2,1,0:T(8,128)(2,1)}, u32[]{:S(2)}, u32[]{:S(2)}) %all-to-all-start.3) | async-done | bytes 3670048 | tf_op jit(solution)/shard_map/all_to_all | solution.py:462
  269.1 5.8 %combine.1 = bf16[256,1536]{1,0:T(8,128)(2,1)} custom-call(bf16[64,224,128]{2,1,0:T(8,128)(2,1)} %all-to-all-done.3.x_hbm, s32[512,1]{1,0:T(8,128)S(1)} %bitcast.47, s32[512,1]{1,0:T(8,128)S(1)} %bitcast.48, f32[256,2]{1,0:T(8,128)S(1)} %bitcast.50, f32[256,1536]{1,0:T(8,128)S(1)} %copy-done.3), custom_call_target="tpu_custom_call" | custom-call | tf_op jit(solution)/shard_map/combine/pallas_call | solution.py:389
  (34 shorter events, 1.1 us)
Async XLA Ops:
  6.5 1.2 copy-start
  6.5 100.5 %all-gather.2.cloned.1.call-start = ((), (), s32[]{:S(2)}) async-start(), calls=%async_computation.4 | async-start | bytes 14266368 | tf_op jit(solution)/shard_map/all_gather | solution.py:427
  11.6 51.0 %copy-start.6 = (f32[1536]{0:T(1024)S(1)}, f32[1536]{0:T(1024)}, u32[]{:S(2)}) copy-start(f32[1536]{0:T(1024)} %param.20) | copy-start | bytes 18436
  11.6 51.0 %copy-start.7 = (f32[1536]{0:T(1024)S(1)}, f32[1536]{0:T(1024)}, u32[]{:S(2)}) copy-start(f32[1536]{0:T(1024)} %param.23) | copy-start | bytes 18436
  11.6 51.0 %copy-start.5 = (s32[1,1,256,2]{2,3,1,0:T(2,128)S(1)}, s32[1,1,256,2]{2,3,1,0:T(2,128)}, u32[]{:S(2)}) copy-start(s32[1,1,256,2]{2,3,1,0:T(2,128)} %param.24) | copy-start | bytes 6148
  11.6 37.8 %all-to-all-start = ((bf16[16,48,1536]{2,1,0:T(8,128)(2,1)}), bf16[16,48,1536]{2,1,0:T(8,128)(2,1)S(1)}, u32[]{:S(2)}, u32[]{:S(2)}) async-start(bf16[16,48,1536]{2,1,0:T(8,128)(2,1)} %pad_maximum_fusion), calls=%async_computation | async-start | bytes 4718592 | tf_op jit(solution)/shard_map/all_to_all | solution.py:433
  54.6 20.1 %all-to-all-start.1 = ((bf16[16,16,1536]{2,1,0:T(8,128)(2,1)}), bf16[16,16,1536]{2,1,0:T(8,128)(2,1)S(1)}, u32[]{:S(2)}, u32[]{:S(2)}) async-start(bf16[16,16,1536]{2,1,0:T(8,128)(2,1)} %time_attention.1), calls=%async_computation.1 | async-start | bytes 1572864 | tf_op jit(solution)/shard_map/all_to_all | solution.py:435
  74.7 1.1 copy-start.4
  123.4 1.2 copy-start.2
  177.0 8.7 %collective-permute-start = (bf16[64,224,128]{2,1,0:T(8,128)(2,1)S(1)}, bf16[64,224,128]{2,1,0:T(8,128)(2,1)S(1)}, u32[]{:S(2)}, u32[]{:S(2)}) collective-permute-start(bf16[64,224,128]{2,1,0:T(8,128)(2,1)S(1)} %all_to_all.20.x_ref), channel_id=1, source_target_pairs={{0,1},{1,0},{2,3},{3,2},{4,5},{5,4},{6,7},{7,6},{8,9},{9,8},{10,11... | collective-permute-start | bytes 11010056 | tf_op jit(solution)/shard_map/ppermute | solution.py:453
  198.1 6.8 %collective-permute-start.1 = (bf16[32,224,128]{2,1,0:T(8,128)(2,1)S(1)}, bf16[32,224,128]{2,1,0:T(8,128)(2,1)S(1)}, u32[]{:S(2)}, u32[]{:S(2)}) collective-permute-start(bf16[32,224,128]{2,1,0:T(8,128)(2,1)S(1)} %experts.5), channel_id=1, source_target_pairs={{0,1},{1,0},{2,3},{3,2},{4,5},{5,4},{6,7},{7,6},{8,9},{9,8},{10,11... | collective-permute-start | bytes 5505032 | tf_op jit(solution)/shard_map/ppermute | solution.py:457
  198.7 6.2 %collective-permute-start.2 = (bf16[32,224,128]{2,1,0:T(8,128)(2,1)S(1)}, bf16[32,224,128]{2,1,0:T(8,128)(2,1)S(1)}, u32[]{:S(2)}, u32[]{:S(2)}) collective-permute-start(bf16[32,224,128]{2,1,0:T(8,128)(2,1)S(1)} %experts.7), channel_id=1, source_target_pairs={{0,1},{1,0},{2,3},{3,2},{4,5},{5,4},{6,7},{7,6},{8,9},{9,8},{10,11... | collective-permute-start | bytes 5505032 | tf_op jit(solution)/shard_map/ppermute | solution.py:459
  207.5 10.5 %copy-start.8 = (f32[1,1,256,2]{2,3,1,0:T(2,128)S(1)}, f32[1,1,256,2]{2,3,1,0:T(2,128)}, u32[]{:S(2)}) copy-start(f32[1,1,256,2]{2,3,1,0:T(2,128)} %param.25) | copy-start | bytes 6148
  207.5 61.6 %copy-start.3 = (f32[256,1536]{1,0:T(8,128)S(1)}, f32[256,1536]{1,0:T(8,128)}, u32[]{:S(2)}) copy-start(f32[256,1536]{1,0:T(8,128)} %copy-done.2) | copy-start | bytes 4718596
  207.5 61.6 %all-to-all-start.3 = ((bf16[64,224,128]{2,1,0:T(8,128)(2,1)}), bf16[64,224,128]{2,1,0:T(8,128)(2,1)}, u32[]{:S(2)}, u32[]{:S(2)}) async-start(bf16[64,224,128]{2,1,0:T(8,128)(2,1)} %add_parts.1), calls=%async_computation.3 | async-start | bytes 7340032 | tf_op jit(solution)/shard_map/all_to_all | solution.py:462
  218.0 57.0 %copy-start.1 = (bf16[1536,288]{0,1:T(8,128)(2,1)S(1)}, bf16[1536,288]{0,1:T(8,128)(2,1)}, u32[]{:S(2)}) copy-start(bf16[1536,288]{0,1:T(8,128)(2,1)} %param.21) | copy-start | bytes 2654212
Sparse Core Ops, SparseCore 0:
  10.4 96.5 all-gather.1

commit v4 on v3

--- a/solution.py
+++ b/solution.py
@@ -142,8 +142,8 @@
             rows_ref[at : at + 16, j * 128 : (j + 1) * 128] = last[j * 16 : (j + 1) * 16, :]
 
 
-GROUPS = ((0, 1, 5, 6, 10, 11), (2, 7, 12, 13), (3, 8, 9, 14), (4, 15))
-QUARTER = D // len(GROUPS)
+GROUPS = 4
+PAIRS = 4
 
 
 def space_kernel(
@@ -158,39 +158,49 @@
     send_ref,
     w_rows,
     merge,
+    projected,
     spatial,
+    total,
     sems,
 ):
+    per_group = FRAMES // GROUPS
+    wide = per_group * 288
+
     def fetch(group, frame, z):
+        f = group * per_group + frame
         return pltpu.make_async_copy(
-            w_hbm.at[frame, z],
-            w_rows.at[pl.ds(frame * 288, 288), pl.ds(z * 384, 384)],
+            w_hbm.at[f, z],
+            w_rows.at[pl.ds(f * 288, 288), pl.ds(z * 384, 384)],
             sems.at[group],
         )
 
-    pieces = [[(frame, z) for frame in frames for z in range(4)] for frames in GROUPS]
-    for group in range(len(GROUPS)):
-        for count, (frame, z) in enumerate(pieces[group]):
-            fetch(group, frame, z).start(priority=count % 2)
-    fetch_merge = pltpu.make_async_copy(merge_hbm, merge, sems.at[len(GROUPS)])
+    pieces = [(frame, z) for frame in range(per_group) for z in range(4)]
+    for group in range(GROUPS):
+        for frame, z in pieces:
+            fetch(group, frame, z).start()
+    fetch_merge = pltpu.make_async_copy(merge_hbm, merge, sems.at[GROUPS])
     fetch_merge.start()
-    for group in range(len(GROUPS)):
-        for frame, z in pieces[group]:
+    for group in range(GROUPS):
+        for frame, z in pieces:
             fetch(group, frame, z).wait()
-        q_all, k_all, v_all = (
-            dot_nt(
-                normed_ref[...], w_rows[part * D + group * QUARTER : part * D + (group + 1) * QUARTER]
-            ).astype(BF16)
-            for part in range(3)
-        )
-        for pair in range(QUARTER // 128):
-            lanes = slice(pair * 128, (pair + 1) * 128)
-            q, k, v = q_all[:, lanes], k_all[:, lanes], v_all[:, lanes]
-            at = group * QUARTER + pair * 128
-            spatial[:, at : at + 128] = attend_pair(q, k, v)
+        rows = slice(group * wide, (group + 1) * wide)
+        projected[:, rows] = dot_nt(normed_ref[...], w_rows[rows, :]).astype(BF16)
+
+    def heads(step, carry):
+        for pair in range(PAIRS):
+            first = pl.multiple_of((step * PAIRS + pair) * 128, 128)
+            q, k, v = (
+                projected[:, pl.ds(pl.multiple_of(first + part * D, 128), 128)] for part in range(3)
+            )
+            spatial[:, pl.ds(first, 128)] = attend_pair(q, k, v)
+        return carry
+
+    lax.fori_loop(0, BLOCKS // PAIRS, heads, 0)
     fetch_merge.wait()
     after_space = after_ref[...] + dot(spatial[...], merge[...])
-    space_ref[...] = after_space
+    total[...] = after_space
+    keep = pltpu.make_async_copy(total, space_ref, sems.at[GROUPS + 1])
+    keep.start()
     mixed_in = norm_rows(after_space, gain_ref[...])
     slot = lax.broadcasted_iota(jnp.int32, (512, ROWS), 0)
     chosen = (slot == main_ref[0:1, :]) | (slot == main_ref[1:2, :])
@@ -209,6 +219,7 @@
         packed = dot(spread, tall).astype(BF16).reshape(8, 32, 128)
         for copy in range(2):
             send_ref[group * 8 : (group + 1) * 8, copy, 192:224, :] = packed
+    keep.wait()
 
 
 def space_step(normed, w_rows, w_merge, after_time, gain, main, last):
@@ -217,16 +228,18 @@
     return pl.pallas_call(
         space_kernel,
         in_specs=[resident, anywhere, anywhere] + [resident] * 4,
-        out_specs=[resident] * 2,
+        out_specs=[anywhere, resident],
         out_shape=[
-            pltpu.VMEM((ROWS, D), F32),
+            pltpu.HBM((ROWS, D), F32),
             pltpu.VMEM((EXPERTS, 2, PACK, 128), BF16),
         ],
         scratch_shapes=[
             pltpu.VMEM((3 * D, D), BF16),
             pltpu.VMEM((D, D), BF16),
+            pltpu.VMEM((ROWS, 3 * D), BF16),
             pltpu.VMEM((ROWS, D), BF16),
-            pltpu.SemaphoreType.DMA((len(GROUPS) + 1,)),
+            pltpu.VMEM((ROWS, D), F32),
+            pltpu.SemaphoreType.DMA((GROUPS + 2,)),
         ],
         compiler_params=pltpu.CompilerParams(vmem_limit_bytes=32 << 20),
         name="space_attention",
@@ -242,17 +255,6 @@
 EXPERT_ROWS = CHUNKS * 18
 CUT = 512
 CUTS = D // CUT
-
-
-def first_kernel(half, x_ref, expand_hbm, reduce_hbm, o_ref, expand, reduce, rows, hidden, sems):
-    def fetch(n):
-        cols = pl.ds((n % CUTS) * CUT, CUT)
-        source, target = (expand_hbm, expand) if n < CUTS else (reduce_hbm, reduce)
-        return pltpu.make_async_copy(source.at[:, :, cols], target.at[:, :, cols], sems.at[n])
-
-    for n in range(2 * CUTS):
-        fetch(n).start()
-    expert_body(half, x_ref, expand, reduce, o_ref, rows, hidden, lambda n: fetch(n).wait())
 
 
 def later_kernel(half, x_ref, expand, reduce, o_ref, rows, hidden):
@@ -328,22 +330,28 @@
 RESIDENT = pl.BlockSpec(memory_space=pltpu.VMEM)
 
 
-def first_experts(arrived, expand, reduce):
+def fetch_kernel(after_ref, expand_hbm, reduce_hbm, expand, reduce, sems):
+    copies = [
+        pltpu.make_async_copy(source, target, sems.at[i])
+        for i, (source, target) in enumerate(((expand_hbm, expand), (reduce_hbm, reduce)))
+    ]
+    for copy in copies:
+        copy.start()
+    for copy in copies:
+        copy.wait()
+
+
+def fetch_weights(after, expand, reduce):
     anywhere = pl.BlockSpec(memory_space=pl.ANY)
     return pl.pallas_call(
-        partial(first_kernel, 0),
-        in_specs=[RESIDENT, anywhere, anywhere],
-        out_specs=[RESIDENT] * 3,
-        out_shape=[
-            pltpu.VMEM(HALF, BF16),
-            pltpu.VMEM((1, D, D), BF16),
-            pltpu.VMEM((1, D, D), BF16),
-        ],
-        scratch_shapes=EXPERT_SCRATCH + [pltpu.SemaphoreType.DMA((2 * CUTS,))],
-        compiler_params=pltpu.CompilerParams(vmem_limit_bytes=16 << 20),
-        cost_estimate=EXPERT_COST,
-        name="experts",
-    )(in_vmem(arrived), in_hbm(expand), in_hbm(reduce))
+        fetch_kernel,
+        in_specs=[anywhere] * 3,
+        out_specs=[RESIDENT] * 2,
+        out_shape=[pltpu.VMEM((1, D, D), BF16)] * 2,
+        scratch_shapes=[pltpu.SemaphoreType.DMA((2,))],
+        compiler_params=pltpu.CompilerParams(vmem_limit_bytes=1 << 20),
+        name="fetch_weights",
+    )(after, in_hbm(expand), in_hbm(reduce))
 
 
 def run_experts(half, arrived, expand, reduce):
@@ -437,6 +445,9 @@
         mixed.reshape(ROWS, D), patches.reshape(ROWS, D), w_time, gain_space.reshape(1, D)
     )
 
+    expand, reduce = fetch_weights(normed, w_expand, w_reduce)
+    normed, expand, reduce = lax.optimization_barrier((normed, expand, reduce))
+
     experts = expert_ids.reshape(ROWS * 2)
     index = jnp.arange(ROWS * 2, dtype=jnp.int32)
     earlier = (experts[:, None] == experts[None, :]) & (index[None, :] < index[:, None])
@@ -451,7 +462,7 @@
         outgoing.reshape(64, PACK, 128), chip_axes, split_axis=0, concat_axis=0, tiled=True
     )
     theirs = lax.ppermute(arrived, "c", swap)
-    part_own, expand, reduce = first_experts(arrived, w_expand, w_reduce)
+    part_own = run_experts(0, arrived, expand, reduce)
     theirs, part_own = lax.optimization_barrier((theirs, part_own))
     part_a = run_experts(0, theirs, expand, reduce)
     back_a = lax.ppermute(part_a, "c", swap)

time: 286 us -> 278 us (0.972); the launches traced: 282 us -> 277 us
  waiting for transfers between devices: 119 us -> 111 us
  local copies, waits for them, and re-layouts: 5.15 us -> 8.81 us
    all_gather x1, waiting for transfers between devices: 27.1 us -> 18.4 us  [shards(): w_rows = lax.all_gather(own_rows, ('x', 'y', 'z', 'c'), axis=0, tiled=True)]
    pallas_call x3 -> x4, Pallas kernels: 18.5 us -> 24.6 us  [run_experts(): pl.pallas_call(partial(later_kernel, half), in_specs=[RESIDENT] * 3, out_...]
    pallas_call x1, Pallas kernels: 8.68 us -> 3.8 us  [fetch_weights(): pl.pallas_call(fetch_kernel, in_specs=[anywhere] * 3, out_specs=[RESIDENT...]
    unnamed x24 -> x30, local copies, waits for them, and re-layouts: 4.12 us -> 7.77 us
  transfers between devices with their start and end apart: 7 -> 7, of which waited for: 4 -> 5; matrix products, arithmetic and copies ran while one was open for 2% -> 2% of each run, Pallas kernels for 9% -> 9%
where the time goes in v4:
time: 278 us; the launch traced here: 277 us
  waiting for transfers between devices  111 us (40%)
  Pallas kernels  61 us (22%)
  blocking collectives  52.6 us (19%)
  starting transfers between devices  26.3 us (9%)
  between operations  14.3 us (5%)
  local copies, waits for them, and re-layouts  8.81 us (3%)
  other arithmetic  3.44 us (1%)
    all_to_all x1, blocking collectives, shards(): lax.all_to_all(outgoing.reshape(64, PACK, 128), chip_axes, split_axis=0,...  52.6 us
    all_to_all x1, waiting for transfers between devices, shards(): lax.all_to_all(sums, chip_axes, split_axis=0, concat_axis=0, tiled=True)  50.9 us
    all_to_all x1, waiting for transfers between devices, shards(): lax.all_to_all(qkv_own, frame_axes, split_axis=0, concat_axis=0, tiled=True)  29.8 us
    pallas_call x4, Pallas kernels, run_experts(): pl.pallas_call(partial(later_kernel, half), in_specs=[RESIDENT] * 3, out_...  24.6 us
    all_gather x1, waiting for transfers between devices, shards(): w_rows = lax.all_gather(own_rows, ('x', 'y', 'z', 'c'), axis=0, tiled=True)  18.4 us
    pallas_call x1, Pallas kernels, space_step(): pl.pallas_call(space_kernel, in_specs=[resident, anywhere, anywhere] + [r...  14.9 us
    all_to_all x1, waiting for transfers between devices, shards(): lax.all_to_all(mixed, frame_axes, split_axis=0, concat_axis=0, tiled=True)  11.3 us
    all_to_all x1, starting transfers between devices, shards(): lax.all_to_all(sums, chip_axes, split_axis=0, concat_axis=0, tiled=True)  10.4 us
  transfers between devices with their start and end apart: 7, of which 5 were waited for; matrix products, arithmetic and copies ran while one was open for 2% of the time, Pallas kernels for 9%

profile of v4, /device:TPU:82, one launch (start us, length us, event | category | flops | bytes accessed | tf_op | source)
XLA Modules:
  0.0 277.3 jit_solution(5853698567734374982)
XLA Ops:
  6.5 1.2 copy-done
  7.7 0.7 dynamic-slice_bitcast_fusion
  8.4 3.2 %pad_maximum_fusion = bf16[16,48,1536]{2,1,0:T(8,128)(2,1)} fusion(bf16[16,16,1536]{2,1,0:T(8,128)(2,1)} %bitcast.52, bf16[16,16,1536]{2,1,0:T(8,128)(2,1)} %bitcast.53, bf16[16,16,1536]{2,1,0:T(8,128)(2,1)} %bitcast.54), kind=kLoop, calls=%fused_computation | loop fusion | flops 7077888 | bytes 4718592 | tf_op jit(solution)/shard_map/concatenate | solution.py:438
  11.6 7.4 %all-to-all-start = ((bf16[16,48,1536]{2,1,0:T(8,128)(2,1)}), bf16[16,48,1536]{2,1,0:T(8,128)(2,1)S(1)}, u32[]{:S(2)}, u32[]{:S(2)}) async-start(bf16[16,48,1536]{2,1,0:T(8,128)(2,1)} %pad_maximum_fusion), calls=%async_computation | async-start | bytes 4718592 | tf_op jit(solution)/shard_map/all_to_all | solution.py:441
  19.6 29.8 %all-to-all-done.x_ref = bf16[16,48,1536]{2,1,0:T(8,128)(2,1)S(1)} async-done(((bf16[16,48,1536]{2,1,0:T(8,128)(2,1)}), bf16[16,48,1536]{2,1,0:T(8,128)(2,1)S(1)}, u32[]{:S(2)}, u32[]{:S(2)}) %all-to-all-start) | async-done | bytes 2359328 | tf_op jit(solution)/shard_map/all_to_all | solution.py:441
  49.4 5.2 %time_attention.1 = bf16[16,16,1536]{2,1,0:T(8,128)(2,1)} custom-call(s32[1]{0:T(128)S(6)} %copy.36.len_ref, bf16[16,48,1536]{2,1,0:T(8,128)(2,1)S(1)} %all-to-all-done.x_ref), custom_call_target="tpu_custom_call" | custom-call | tf_op jit(solution)/shard_map/time_attention/pallas_call | solution.py:84
  54.6 7.9 %all-to-all-start.1 = ((bf16[16,16,1536]{2,1,0:T(8,128)(2,1)}), bf16[16,16,1536]{2,1,0:T(8,128)(2,1)S(1)}, u32[]{:S(2)}, u32[]{:S(2)}) async-start(bf16[16,16,1536]{2,1,0:T(8,128)(2,1)} %time_attention.1), calls=%async_computation.1 | async-start | bytes 1572864 | tf_op jit(solution)/shard_map/all_to_all | solution.py:443
  63.4 11.3 %all-to-all-done.1 = bf16[16,16,1536]{2,1,0:T(8,128)(2,1)S(1)} async-done(((bf16[16,16,1536]{2,1,0:T(8,128)(2,1)}), bf16[16,16,1536]{2,1,0:T(8,128)(2,1)S(1)}, u32[]{:S(2)}, u32[]{:S(2)}) %all-to-all-start.1) | async-done | bytes 786464 | tf_op jit(solution)/shard_map/all_to_all | solution.py:443
  74.7 1.1 copy-done.3
  75.8 4.1 %after_time.1 = (f32[256,1536]{1,0:T(8,128)S(1)}, bf16[256,1536]{1,0:T(8,128)(2,1)S(1)}) custom-call(bf16[256,1536]{1,0:T(8,128)(2,1)S(1)} %bitcast.46, bf16[256,1536]{1,0:T(8,128)(2,1)S(1)} %bitcast.49, bf16[1536,1536]{1,0:T(8,128)(2,1)} %w_ref.1, f32[1,1536]{1,0:T(1,128)S(1)} %reshape.57.gain_ref), custom_call_target="tpu_custom_call" | custom-call | tf_op jit(solution)/shard_map/after_time/pallas_call | solution.py:103
  79.9 3.8 %fetch_weights.1 = (bf16[1,1536,1536]{2,1,0:T(8,128)(2,1)S(1)}, bf16[1,1536,1536]{2,1,0:T(8,128)(2,1)S(1)}) custom-call(bf16[256,1536]{1,0:T(8,128)(2,1)S(1)} %get-tuple-element.19.after_ref.normed_ref, bf16[1,1536,1536]{2,1,0:T(8,128)(2,1)} %expand_hbm.1, bf16[1,1536,1536]{2,1,0:T(8,128)(2,1)} %reduce_hbm.1), custom_call_target="tpu_custom_call" | custom-call | tf_op jit(solution)/shard_map/fetch_weights/pallas_call | solution.py:346
  83.8 2.7 copy-done.4
  86.4 2.2 copy-done.6
  88.6 18.4 %all-gather.2.cloned.1.call-done = bf16[18432,384]{1,0:T(8,128)(2,1)} async-done(((bf16[144,384]{1,0:T(8,128)(2,1)}), bf16[18432,384]{1,0:T(8,128)(2,1)}) %all-gather.2.cloned.1.call-update) | async-done | bytes 14155792 | tf_op jit(solution)/shard_map/all_gather | solution.py:435
  107.0 14.9 %space_attention.1 = (f32[256,1536]{1,0:T(8,128)}, bf16[32,2,224,128]{3,2,1,0:T(8,128)(2,1)S(1)}) custom-call(bf16[256,1536]{1,0:T(8,128)(2,1)S(1)} %get-tuple-element.19.after_ref.normed_ref, bf16[16,4,288,384]{3,2,1,0:T(8,128)(2,1)} %bitcast.51, bf16[1536,1536]{1,0:T(8,128)(2,1)} %merge_hbm.1, f32[256,1536]{1,0:T(8,128)S(1)} %get-tuple-element.20.after_ref, ...), custom_call_target="tpu_custom_call" | custom-call | tf_op jit(solution)/shard_map/space_attention/pallas_call | solution.py:228
  121.9 52.6 %all_to_all.20.x_ref = bf16[64,224,128]{2,1,0:T(8,128)(2,1)S(1)} all-to-all(bf16[64,224,128]{2,1,0:T(8,128)(2,1)S(1)} %bitcast.45), channel_id=1, replica_groups=mesh['x'=4,'y'=4,'z'=4,'c'=2] {'x','y','z'}, dimensions={0} | all-to-all | bytes 7340032 | tf_op jit(solution)/shard_map/all_to_all | solution.py:461
  174.5 6.1 %experts.4.own_a = bf16[32,224,128]{2,1,0:T(8,128)(2,1)S(1)} custom-call(bf16[64,224,128]{2,1,0:T(8,128)(2,1)S(1)} %all_to_all.20.x_ref, bf16[1,1536,1536]{2,1,0:T(8,128)(2,1)S(1)} %copy-done.5, bf16[1,1536,1536]{2,1,0:T(8,128)(2,1)S(1)} %copy-done.7), custom_call_target="tpu_custom_call" | custom-call | flops 5435817984 | bytes 3670016 | tf_op jit(solution)/shard_map/experts/pallas_call | solution.py:358
  180.9 6.1 %experts.7 = bf16[32,224,128]{2,1,0:T(8,128)(2,1)S(1)} custom-call(bf16[64,224,128]{2,1,0:T(8,128)(2,1)S(1)} %collective-permute-done.x_ref, bf16[1,1536,1536]{2,1,0:T(8,128)(2,1)S(1)} %copy-done.5, bf16[1,1536,1536]{2,1,0:T(8,128)(2,1)S(1)} %copy-done.7), custom_call_target="tpu_custom_call" | custom-call | flops 5435817984 | bytes 3670016 | tf_op jit(solution)/shard_map/experts/pallas_call | solution.py:358
  187.0 6.3 %experts.5 = bf16[32,224,128]{2,1,0:T(8,128)(2,1)S(1)} custom-call(bf16[64,224,128]{2,1,0:T(8,128)(2,1)S(1)} %collective-permute-done.x_ref, bf16[1,1536,1536]{2,1,0:T(8,128)(2,1)S(1)} %copy-done.5, bf16[1,1536,1536]{2,1,0:T(8,128)(2,1)S(1)} %copy-done.7), custom_call_target="tpu_custom_call" | custom-call | flops 5435817984 | bytes 3670016 | tf_op jit(solution)/shard_map/experts/pallas_call | solution.py:358
  193.9 6.1 %experts.6.own_b = bf16[32,224,128]{2,1,0:T(8,128)(2,1)S(1)} custom-call(bf16[64,224,128]{2,1,0:T(8,128)(2,1)S(1)} %all_to_all.20.x_ref, bf16[1,1536,1536]{2,1,0:T(8,128)(2,1)S(1)} %copy-done.5, bf16[1,1536,1536]{2,1,0:T(8,128)(2,1)S(1)} %copy-done.7), custom_call_target="tpu_custom_call" | custom-call | flops 5435817984 | bytes 3670016 | tf_op jit(solution)/shard_map/experts/pallas_call | solution.py:358
  200.0 2.6 add_parts.1
  202.7 10.4 %all-to-all-start.3 = ((bf16[64,224,128]{2,1,0:T(8,128)(2,1)}), bf16[64,224,128]{2,1,0:T(8,128)(2,1)}, u32[]{:S(2)}, u32[]{:S(2)}) async-start(bf16[64,224,128]{2,1,0:T(8,128)(2,1)} %add_parts.1), calls=%async_computation.3 | async-start | bytes 7340032 | tf_op jit(solution)/shard_map/all_to_all | solution.py:473
  213.6 50.9 %all-to-all-done.3.x_hbm = bf16[64,224,128]{2,1,0:T(8,128)(2,1)} async-done(((bf16[64,224,128]{2,1,0:T(8,128)(2,1)}), bf16[64,224,128]{2,1,0:T(8,128)(2,1)}, u32[]{:S(2)}, u32[]{:S(2)}) %all-to-all-start.3) | async-done | bytes 3670048 | tf_op jit(solution)/shard_map/all_to_all | solution.py:473
  264.6 5.8 %combine.1 = bf16[256,1536]{1,0:T(8,128)(2,1)} custom-call(bf16[64,224,128]{2,1,0:T(8,128)(2,1)} %all-to-all-done.3.x_hbm, s32[512,1]{1,0:T(8,128)S(1)} %bitcast.47, s32[512,1]{1,0:T(8,128)S(1)} %bitcast.48, f32[256,2]{1,0:T(8,128)S(1)} %bitcast.50, f32[256,1536]{1,0:T(8,128)S(1)} %copy-done.2), custom_call_target="tpu_custom_call" | custom-call | tf_op jit(solution)/shard_map/combine/pallas_call | solution.py:397
  (41 shorter events, 2.2 us)
Async XLA Ops:
  6.5 1.2 copy-start
  6.5 100.5 %all-gather.2.cloned.1.call-start = ((), (), s32[]{:S(2)}) async-start(), calls=%async_computation.4 | async-start | bytes 14266368 | tf_op jit(solution)/shard_map/all_gather | solution.py:435
  11.6 51.0 %copy-start.9 = (f32[1536]{0:T(1024)S(1)}, f32[1536]{0:T(1024)}, u32[]{:S(2)}) copy-start(f32[1536]{0:T(1024)} %param.20) | copy-start | bytes 18436
  11.6 51.0 %copy-start.8 = (s32[1,1,256,2]{2,3,1,0:T(2,128)S(1)}, s32[1,1,256,2]{2,3,1,0:T(2,128)}, u32[]{:S(2)}) copy-start(s32[1,1,256,2]{2,3,1,0:T(2,128)} %param.24) | copy-start | bytes 6148
  11.6 37.8 %all-to-all-start = ((bf16[16,48,1536]{2,1,0:T(8,128)(2,1)}), bf16[16,48,1536]{2,1,0:T(8,128)(2,1)S(1)}, u32[]{:S(2)}, u32[]{:S(2)}) async-start(bf16[16,48,1536]{2,1,0:T(8,128)(2,1)} %pad_maximum_fusion), calls=%async_computation | async-start | bytes 4718592 | tf_op jit(solution)/shard_map/all_to_all | solution.py:441
  19.0 44.4 %copy-start.10 = (f32[1536]{0:T(1024)S(1)}, f32[1536]{0:T(1024)}, u32[]{:S(2)}) copy-start(f32[1536]{0:T(1024)} %param.23) | copy-start | bytes 18436
  54.6 20.1 %all-to-all-start.1 = ((bf16[16,16,1536]{2,1,0:T(8,128)(2,1)}), bf16[16,16,1536]{2,1,0:T(8,128)(2,1)S(1)}, u32[]{:S(2)}, u32[]{:S(2)}) async-start(bf16[16,16,1536]{2,1,0:T(8,128)(2,1)} %time_attention.1), calls=%async_computation.1 | async-start | bytes 1572864 | tf_op jit(solution)/shard_map/all_to_all | solution.py:443
  74.7 1.1 copy-start.3
  83.7 2.7 copy-start.4
  86.4 2.2 copy-start.6
  107.0 67.5 %copy-start.7 = (bf16[1,1536,1536]{2,1,0:T(8,128)(2,1)S(1)}, bf16[1,1536,1536]{2,1,0:T(8,128)(2,1)}, u32[]{:S(2)}) copy-start(bf16[1,1536,1536]{2,1,0:T(8,128)(2,1)} %copy-done.6) | copy-start | bytes 14155780
  121.9 52.6 %copy-start.5 = (bf16[1,1536,1536]{2,1,0:T(8,128)(2,1)S(1)}, bf16[1,1536,1536]{2,1,0:T(8,128)(2,1)}, u32[]{:S(2)}) copy-start(bf16[1,1536,1536]{2,1,0:T(8,128)(2,1)} %copy-done.4) | copy-start | bytes 14155780
  174.5 6.4 %collective-permute-start = (bf16[64,224,128]{2,1,0:T(8,128)(2,1)S(1)}, bf16[64,224,128]{2,1,0:T(8,128)(2,1)S(1)}, u32[]{:S(2)}, u32[]{:S(2)}) collective-permute-start(bf16[64,224,128]{2,1,0:T(8,128)(2,1)S(1)} %all_to_all.20.x_ref), channel_id=1, source_target_pairs={{0,1},{1,0},{2,3},{3,2},{4,5},{5,4},{6,7},{7,6},{8,9},{9,8},{10,11... | collective-permute-start | bytes 11010056 | tf_op jit(solution)/shard_map/ppermute | solution.py:464
  193.3 6.7 %collective-permute-start.2 = (bf16[32,224,128]{2,1,0:T(8,128)(2,1)S(1)}, bf16[32,224,128]{2,1,0:T(8,128)(2,1)S(1)}, u32[]{:S(2)}, u32[]{:S(2)}) collective-permute-start(bf16[32,224,128]{2,1,0:T(8,128)(2,1)S(1)} %experts.7), channel_id=1, source_target_pairs={{0,1},{1,0},{2,3},{3,2},{4,5},{5,4},{6,7},{7,6},{8,9},{9,8},{10,11... | collective-permute-start | bytes 5505032 | tf_op jit(solution)/shard_map/ppermute | solution.py:470
  193.6 6.4 %collective-permute-start.1 = (bf16[32,224,128]{2,1,0:T(8,128)(2,1)S(1)}, bf16[32,224,128]{2,1,0:T(8,128)(2,1)S(1)}, u32[]{:S(2)}, u32[]{:S(2)}) collective-permute-start(bf16[32,224,128]{2,1,0:T(8,128)(2,1)S(1)} %experts.5), channel_id=1, source_target_pairs={{0,1},{1,0},{2,3},{3,2},{4,5},{5,4},{6,7},{7,6},{8,9},{9,8},{10,11... | collective-permute-start | bytes 5505032 | tf_op jit(solution)/shard_map/ppermute | solution.py:468
  202.7 10.8 %copy-start.11 = (f32[1,1,256,2]{2,3,1,0:T(2,128)S(1)}, f32[1,1,256,2]{2,3,1,0:T(2,128)}, u32[]{:S(2)}) copy-start(f32[1,1,256,2]{2,3,1,0:T(2,128)} %param.25) | copy-start | bytes 6148
  202.7 61.9 %copy-start.2 = (f32[256,1536]{1,0:T(8,128)S(1)}, f32[256,1536]{1,0:T(8,128)}, u32[]{:S(2)}) copy-start(f32[256,1536]{1,0:T(8,128)} %get-tuple-element.26.space_ref) | copy-start | bytes 4718596
  202.7 61.9 %all-to-all-start.3 = ((bf16[64,224,128]{2,1,0:T(8,128)(2,1)}), bf16[64,224,128]{2,1,0:T(8,128)(2,1)}, u32[]{:S(2)}, u32[]{:S(2)}) async-start(bf16[64,224,128]{2,1,0:T(8,128)(2,1)} %add_parts.1), calls=%async_computation.3 | async-start | bytes 7340032 | tf_op jit(solution)/shard_map/all_to_all | solution.py:473
  213.1 57.3 %copy-start.1 = (bf16[1536,288]{0,1:T(8,128)(2,1)S(1)}, bf16[1536,288]{0,1:T(8,128)(2,1)}, u32[]{:S(2)}) copy-start(bf16[1536,288]{0,1:T(8,128)(2,1)} %param.21) | copy-start | bytes 2654212
Sparse Core Ops, SparseCore 0:
  10.4 96.5 all-gather.1

commit v5 on v4

--- a/solution.py
+++ b/solution.py
@@ -61,6 +61,30 @@
 
 
 TIME_PAIRS = 3
+
+
+def stack_kernel(q_ref, k_ref, v_ref, o_ref, sems):
+    copies = [
+        pltpu.make_async_copy(ref, o_ref.at[:, pl.ds(i * 16, 16), :], sems.at[i])
+        for i, ref in enumerate((q_ref, k_ref, v_ref))
+    ]
+    for copy in copies:
+        copy.start()
+    for copy in copies:
+        copy.wait()
+
+
+def stack_rows(q, k, v):
+    anywhere = pl.BlockSpec(memory_space=pl.ANY)
+    return pl.pallas_call(
+        stack_kernel,
+        in_specs=[anywhere] * 3,
+        out_specs=anywhere,
+        out_shape=pltpu.HBM((FRAMES, 48, D), BF16),
+        scratch_shapes=[pltpu.SemaphoreType.DMA((3,))],
+        compiler_params=pltpu.CompilerParams(vmem_limit_bytes=1 << 20),
+        name="stack_rows",
+    )(*map(in_hbm, (q, k, v)))
 
 
 def time_kernel(len_ref, x_ref, o_ref):
@@ -435,9 +459,7 @@
     w_rows = lax.all_gather(own_rows, ("x", "y", "z", "c"), axis=0, tiled=True)
     w_rows = w_rows.reshape(FRAMES, 4, 288, 384)
 
-    qkv_own = jnp.concatenate(
-        [a.reshape(FRAMES, 16, D) for a in (temporal_q, temporal_k, temporal_v)], axis=1
-    )
+    qkv_own = stack_rows(*(a.reshape(FRAMES, 16, D) for a in (temporal_q, temporal_k, temporal_v)))
     qkv = lax.all_to_all(qkv_own, frame_axes, split_axis=0, concat_axis=0, tiled=True)
     mixed = time_attention(clip_lengths, qkv)
     mixed = lax.all_to_all(mixed, frame_axes, split_axis=0, concat_axis=0, tiled=True)

time: 278 us -> 319 us (1.15)
  Pallas kernels: 61 us -> 134 us
  waiting for transfers between devices: 111 us -> 86.1 us
  blocking collectives: 52.6 us -> 48.6 us
    pallas_call x0 -> x1, Pallas kernels: none -> 72.6 us  [stack_rows(): pl.pallas_call(stack_kernel, in_specs=[anywhere] * 3, out_specs=anywhere,...]
    all_gather x1, waiting for transfers between devices: 18.4 us -> 0.01 us  [shards(): w_rows = lax.all_gather(own_rows, ('x', 'y', 'z', 'c'), axis=0, tiled=True)]
    all_to_all x1, blocking collectives: 52.6 us -> 48.6 us  [shards(): lax.all_to_all(outgoing.reshape(64, PACK, 128), chip_axes, split_axis=0,...]
    all_to_all x1, waiting for transfers between devices: 11.3 us -> 8.04 us  [shards(): lax.all_to_all(mixed, frame_axes, split_axis=0, concat_axis=0, tiled=True)]
  transfers between devices with their start and end apart: 7 -> 7, of which waited for: 5 -> 4; matrix products, arithmetic and copies ran while one was open for 2% -> 0% of each run, Pallas kernels for 9% -> 31%
where the time goes in v5:
time: 319 us; the launch traced here: 318 us
  Pallas kernels  134 us (42%)
  waiting for transfers between devices  86.1 us (27%)
  blocking collectives  48.6 us (15%)
  starting transfers between devices  26.7 us (8%)
  between operations  14.3 us (4%)
  local copies, waits for them, and re-layouts  8.26 us (3%)
    pallas_call x1, Pallas kernels, stack_rows(): pl.pallas_call(stack_kernel, in_specs=[anywhere] * 3, out_specs=anywhere,...  72.6 us
    all_to_all x1, waiting for transfers between devices, shards(): lax.all_to_all(sums, chip_axes, split_axis=0, concat_axis=0, tiled=True)  49.1 us
    all_to_all x1, blocking collectives, shards(): lax.all_to_all(outgoing.reshape(64, PACK, 128), chip_axes, split_axis=0,...  48.6 us
    all_to_all x1, waiting for transfers between devices, shards(): lax.all_to_all(qkv_own, frame_axes, split_axis=0, concat_axis=0, tiled=True)  28.6 us
    pallas_call x4, Pallas kernels, run_experts(): pl.pallas_call(partial(later_kernel, half), in_specs=[RESIDENT] * 3, out_...  24.6 us
    pallas_call x1, Pallas kernels, space_step(): pl.pallas_call(space_kernel, in_specs=[resident, anywhere, anywhere] + [r...  14.9 us
    all_to_all x1, starting transfers between devices, shards(): lax.all_to_all(sums, chip_axes, split_axis=0, concat_axis=0, tiled=True)  11 us
    all_to_all x1, waiting for transfers between devices, shards(): lax.all_to_all(mixed, frame_axes, split_axis=0, concat_axis=0, tiled=True)  8.04 us
  transfers between devices with their start and end apart: 7, of which 4 were waited for; matrix products, arithmetic and copies ran while one was open for 0% of the time, Pallas kernels for 31%

profile of v5, /device:TPU:82, one launch (start us, length us, event | category | flops | bytes accessed | tf_op | source)
XLA Modules:
  0.0 317.9 jit_solution(10233996050937398043)
XLA Ops:
  6.5 1.2 copy-done
  7.7 0.7 dynamic-slice_bitcast_fusion
  8.4 72.6 %stack_rows.1 = bf16[16,48,1536]{2,1,0:T(8,128)(2,1)} custom-call(bf16[16,16,1536]{2,1,0:T(8,128)(2,1)} %bitcast.52, bf16[16,16,1536]{2,1,0:T(8,128)(2,1)} %bitcast.53, bf16[16,16,1536]{2,1,0:T(8,128)(2,1)} %bitcast.54), custom_call_target="tpu_custom_call" | custom-call | tf_op jit(solution)/shard_map/stack_rows/pallas_call | solution.py:79
  81.0 7.3 %all-to-all-start = ((bf16[16,48,1536]{2,1,0:T(8,128)(2,1)}), bf16[16,48,1536]{2,1,0:T(8,128)(2,1)S(1)}, u32[]{:S(2)}, u32[]{:S(2)}) async-start(bf16[16,48,1536]{2,1,0:T(8,128)(2,1)} %stack_rows.1), calls=%async_computation | async-start | bytes 4718592 | tf_op jit(solution)/shard_map/all_to_all | solution.py:463
  89.0 28.6 %all-to-all-done.x_ref = bf16[16,48,1536]{2,1,0:T(8,128)(2,1)S(1)} async-done(((bf16[16,48,1536]{2,1,0:T(8,128)(2,1)}), bf16[16,48,1536]{2,1,0:T(8,128)(2,1)S(1)}, u32[]{:S(2)}, u32[]{:S(2)}) %all-to-all-start) | async-done | bytes 2359328 | tf_op jit(solution)/shard_map/all_to_all | solution.py:463
  117.6 5.2 %time_attention.1 = bf16[16,16,1536]{2,1,0:T(8,128)(2,1)} custom-call(s32[1]{0:T(128)S(6)} %copy.36.len_ref, bf16[16,48,1536]{2,1,0:T(8,128)(2,1)S(1)} %all-to-all-done.x_ref), custom_call_target="tpu_custom_call" | custom-call | tf_op jit(solution)/shard_map/time_attention/pallas_call | solution.py:108
  122.8 7.9 %all-to-all-start.1 = ((bf16[16,16,1536]{2,1,0:T(8,128)(2,1)}), bf16[16,16,1536]{2,1,0:T(8,128)(2,1)S(1)}, u32[]{:S(2)}, u32[]{:S(2)}) async-start(bf16[16,16,1536]{2,1,0:T(8,128)(2,1)} %time_attention.1), calls=%async_computation.1 | async-start | bytes 1572864 | tf_op jit(solution)/shard_map/all_to_all | solution.py:465
  131.5 8.0 %all-to-all-done.1 = bf16[16,16,1536]{2,1,0:T(8,128)(2,1)S(1)} async-done(((bf16[16,16,1536]{2,1,0:T(8,128)(2,1)}), bf16[16,16,1536]{2,1,0:T(8,128)(2,1)S(1)}, u32[]{:S(2)}, u32[]{:S(2)}) %all-to-all-start.1) | async-done | bytes 786464 | tf_op jit(solution)/shard_map/all_to_all | solution.py:465
  139.6 1.1 copy-done.3
  140.7 4.1 %after_time.1 = (f32[256,1536]{1,0:T(8,128)S(1)}, bf16[256,1536]{1,0:T(8,128)(2,1)S(1)}) custom-call(bf16[256,1536]{1,0:T(8,128)(2,1)S(1)} %bitcast.46, bf16[256,1536]{1,0:T(8,128)(2,1)S(1)} %bitcast.49, bf16[1536,1536]{1,0:T(8,128)(2,1)} %w_ref.1, f32[1,1536]{1,0:T(1,128)S(1)} %reshape.57.gain_ref), custom_call_target="tpu_custom_call" | custom-call | tf_op jit(solution)/shard_map/after_time/pallas_call | solution.py:127
  144.8 3.8 %fetch_weights.1 = (bf16[1,1536,1536]{2,1,0:T(8,128)(2,1)S(1)}, bf16[1,1536,1536]{2,1,0:T(8,128)(2,1)S(1)}) custom-call(bf16[256,1536]{1,0:T(8,128)(2,1)S(1)} %get-tuple-element.19.after_ref.normed_ref, bf16[1,1536,1536]{2,1,0:T(8,128)(2,1)} %expand_hbm.1, bf16[1,1536,1536]{2,1,0:T(8,128)(2,1)} %reduce_hbm.1), custom_call_target="tpu_custom_call" | custom-call | tf_op jit(solution)/shard_map/fetch_weights/pallas_call | solution.py:370
  148.6 2.1 copy-done.4
  150.7 2.2 copy-done.6
  152.9 14.9 %space_attention.1 = (f32[256,1536]{1,0:T(8,128)}, bf16[32,2,224,128]{3,2,1,0:T(8,128)(2,1)S(1)}) custom-call(bf16[256,1536]{1,0:T(8,128)(2,1)S(1)} %get-tuple-element.19.after_ref.normed_ref, bf16[16,4,288,384]{3,2,1,0:T(8,128)(2,1)} %bitcast.51, bf16[1536,1536]{1,0:T(8,128)(2,1)} %merge_hbm.1, f32[256,1536]{1,0:T(8,128)S(1)} %get-tuple-element.20.after_ref, ...), custom_call_target="tpu_custom_call" | custom-call | tf_op jit(solution)/shard_map/space_attention/pallas_call | solution.py:252
  167.8 48.6 %all_to_all.20.x_ref = bf16[64,224,128]{2,1,0:T(8,128)(2,1)S(1)} all-to-all(bf16[64,224,128]{2,1,0:T(8,128)(2,1)S(1)} %bitcast.45), channel_id=1, replica_groups=mesh['x'=4,'y'=4,'z'=4,'c'=2] {'x','y','z'}, dimensions={0} | all-to-all | bytes 7340032 | tf_op jit(solution)/shard_map/all_to_all | solution.py:483
  216.5 6.1 %experts.4.own_a = bf16[32,224,128]{2,1,0:T(8,128)(2,1)S(1)} custom-call(bf16[64,224,128]{2,1,0:T(8,128)(2,1)S(1)} %all_to_all.20.x_ref, bf16[1,1536,1536]{2,1,0:T(8,128)(2,1)S(1)} %copy-done.5, bf16[1,1536,1536]{2,1,0:T(8,128)(2,1)S(1)} %copy-done.7), custom_call_target="tpu_custom_call" | custom-call | flops 5435817984 | bytes 3670016 | tf_op jit(solution)/shard_map/experts/pallas_call | solution.py:382
  222.6 0.3 collective-permute-done.x_ref
  222.9 6.1 %experts.7 = bf16[32,224,128]{2,1,0:T(8,128)(2,1)S(1)} custom-call(bf16[64,224,128]{2,1,0:T(8,128)(2,1)S(1)} %collective-permute-done.x_ref, bf16[1,1536,1536]{2,1,0:T(8,128)(2,1)S(1)} %copy-done.5, bf16[1,1536,1536]{2,1,0:T(8,128)(2,1)S(1)} %copy-done.7), custom_call_target="tpu_custom_call" | custom-call | flops 5435817984 | bytes 3670016 | tf_op jit(solution)/shard_map/experts/pallas_call | solution.py:382
  229.0 6.3 %experts.5 = bf16[32,224,128]{2,1,0:T(8,128)(2,1)S(1)} custom-call(bf16[64,224,128]{2,1,0:T(8,128)(2,1)S(1)} %collective-permute-done.x_ref, bf16[1,1536,1536]{2,1,0:T(8,128)(2,1)S(1)} %copy-done.5, bf16[1,1536,1536]{2,1,0:T(8,128)(2,1)S(1)} %copy-done.7), custom_call_target="tpu_custom_call" | custom-call | flops 5435817984 | bytes 3670016 | tf_op jit(solution)/shard_map/experts/pallas_call | solution.py:382
  235.9 6.1 %experts.6.own_b = bf16[32,224,128]{2,1,0:T(8,128)(2,1)S(1)} custom-call(bf16[64,224,128]{2,1,0:T(8,128)(2,1)S(1)} %all_to_all.20.x_ref, bf16[1,1536,1536]{2,1,0:T(8,128)(2,1)S(1)} %copy-done.5, bf16[1,1536,1536]{2,1,0:T(8,128)(2,1)S(1)} %copy-done.7), custom_call_target="tpu_custom_call" | custom-call | flops 5435817984 | bytes 3670016 | tf_op jit(solution)/shard_map/experts/pallas_call | solution.py:382
  242.0 2.6 add_parts.1
  244.6 11.0 %all-to-all-start.3 = ((bf16[64,224,128]{2,1,0:T(8,128)(2,1)}), bf16[64,224,128]{2,1,0:T(8,128)(2,1)}, u32[]{:S(2)}, u32[]{:S(2)}) async-start(bf16[64,224,128]{2,1,0:T(8,128)(2,1)} %add_parts.1), calls=%async_computation.3 | async-start | bytes 7340032 | tf_op jit(solution)/shard_map/all_to_all | solution.py:495
  256.1 49.1 %all-to-all-done.3.x_hbm = bf16[64,224,128]{2,1,0:T(8,128)(2,1)} async-done(((bf16[64,224,128]{2,1,0:T(8,128)(2,1)}), bf16[64,224,128]{2,1,0:T(8,128)(2,1)}, u32[]{:S(2)}, u32[]{:S(2)}) %all-to-all-start.3) | async-done | bytes 3670048 | tf_op jit(solution)/shard_map/all_to_all | solution.py:495
  305.2 5.8 %combine.1 = bf16[256,1536]{1,0:T(8,128)(2,1)} custom-call(bf16[64,224,128]{2,1,0:T(8,128)(2,1)} %all-to-all-done.3.x_hbm, s32[512,1]{1,0:T(8,128)S(1)} %bitcast.47, s32[512,1]{1,0:T(8,128)S(1)} %bitcast.48, f32[256,2]{1,0:T(8,128)S(1)} %bitcast.50, f32[256,1536]{1,0:T(8,128)S(1)} %copy-done.2), custom_call_target="tpu_custom_call" | custom-call | tf_op jit(solution)/shard_map/combine/pallas_call | solution.py:421
  (41 shorter events, 1.9 us)
Async XLA Ops:
  6.5 1.2 copy-start
  6.5 146.4 %all-gather.2.cloned.1.call-start = ((), (), s32[]{:S(2)}) async-start(), calls=%async_computation.4 | async-start | bytes 14266368 | tf_op jit(solution)/shard_map/all_gather | solution.py:459
  81.0 49.7 %copy-start.9 = (f32[1536]{0:T(1024)S(1)}, f32[1536]{0:T(1024)}, u32[]{:S(2)}) copy-start(f32[1536]{0:T(1024)} %param.20) | copy-start | bytes 18436
  81.0 49.7 %copy-start.8 = (s32[1,1,256,2]{2,3,1,0:T(2,128)S(1)}, s32[1,1,256,2]{2,3,1,0:T(2,128)}, u32[]{:S(2)}) copy-start(s32[1,1,256,2]{2,3,1,0:T(2,128)} %param.24) | copy-start | bytes 6148
  81.0 36.6 %all-to-all-start = ((bf16[16,48,1536]{2,1,0:T(8,128)(2,1)}), bf16[16,48,1536]{2,1,0:T(8,128)(2,1)S(1)}, u32[]{:S(2)}, u32[]{:S(2)}) async-start(bf16[16,48,1536]{2,1,0:T(8,128)(2,1)} %stack_rows.1), calls=%async_computation | async-start | bytes 4718592 | tf_op jit(solution)/shard_map/all_to_all | solution.py:463
  88.3 43.2 %copy-start.10 = (f32[1536]{0:T(1024)S(1)}, f32[1536]{0:T(1024)}, u32[]{:S(2)}) copy-start(f32[1536]{0:T(1024)} %param.23) | copy-start | bytes 18436
  122.8 16.8 %all-to-all-start.1 = ((bf16[16,16,1536]{2,1,0:T(8,128)(2,1)}), bf16[16,16,1536]{2,1,0:T(8,128)(2,1)S(1)}, u32[]{:S(2)}, u32[]{:S(2)}) async-start(bf16[16,16,1536]{2,1,0:T(8,128)(2,1)} %time_attention.1), calls=%async_computation.1 | async-start | bytes 1572864 | tf_op jit(solution)/shard_map/all_to_all | solution.py:465
  139.6 1.1 copy-start.3
  148.6 2.1 copy-start.4
  150.7 2.2 copy-start.6
  152.9 63.5 %copy-start.7 = (bf16[1,1536,1536]{2,1,0:T(8,128)(2,1)S(1)}, bf16[1,1536,1536]{2,1,0:T(8,128)(2,1)}, u32[]{:S(2)}) copy-start(bf16[1,1536,1536]{2,1,0:T(8,128)(2,1)} %copy-done.6) | copy-start | bytes 14155780
  167.8 48.6 %copy-start.5 = (bf16[1,1536,1536]{2,1,0:T(8,128)(2,1)S(1)}, bf16[1,1536,1536]{2,1,0:T(8,128)(2,1)}, u32[]{:S(2)}) copy-start(bf16[1,1536,1536]{2,1,0:T(8,128)(2,1)} %copy-done.4) | copy-start | bytes 14155780
  216.5 6.4 %collective-permute-start = (bf16[64,224,128]{2,1,0:T(8,128)(2,1)S(1)}, bf16[64,224,128]{2,1,0:T(8,128)(2,1)S(1)}, u32[]{:S(2)}, u32[]{:S(2)}) collective-permute-start(bf16[64,224,128]{2,1,0:T(8,128)(2,1)S(1)} %all_to_all.20.x_ref), channel_id=1, source_target_pairs={{0,1},{1,0},{2,3},{3,2},{4,5},{5,4},{6,7},{7,6},{8,9},{9,8},{10,11... | collective-permute-start | bytes 11010056 | tf_op jit(solution)/shard_map/ppermute | solution.py:486
  235.3 6.7 %collective-permute-start.2 = (bf16[32,224,128]{2,1,0:T(8,128)(2,1)S(1)}, bf16[32,224,128]{2,1,0:T(8,128)(2,1)S(1)}, u32[]{:S(2)}, u32[]{:S(2)}) collective-permute-start(bf16[32,224,128]{2,1,0:T(8,128)(2,1)S(1)} %experts.7), channel_id=1, source_target_pairs={{0,1},{1,0},{2,3},{3,2},{4,5},{5,4},{6,7},{7,6},{8,9},{9,8},{10,11... | collective-permute-start | bytes 5505032 | tf_op jit(solution)/shard_map/ppermute | solution.py:492
  235.6 6.4 %collective-permute-start.1 = (bf16[32,224,128]{2,1,0:T(8,128)(2,1)S(1)}, bf16[32,224,128]{2,1,0:T(8,128)(2,1)S(1)}, u32[]{:S(2)}, u32[]{:S(2)}) collective-permute-start(bf16[32,224,128]{2,1,0:T(8,128)(2,1)S(1)} %experts.5), channel_id=1, source_target_pairs={{0,1},{1,0},{2,3},{3,2},{4,5},{5,4},{6,7},{7,6},{8,9},{9,8},{10,11... | collective-permute-start | bytes 5505032 | tf_op jit(solution)/shard_map/ppermute | solution.py:490
  244.6 11.3 %copy-start.11 = (f32[1,1,256,2]{2,3,1,0:T(2,128)S(1)}, f32[1,1,256,2]{2,3,1,0:T(2,128)}, u32[]{:S(2)}) copy-start(f32[1,1,256,2]{2,3,1,0:T(2,128)} %param.25) | copy-start | bytes 6148
  244.6 60.6 %copy-start.2 = (f32[256,1536]{1,0:T(8,128)S(1)}, f32[256,1536]{1,0:T(8,128)}, u32[]{:S(2)}) copy-start(f32[256,1536]{1,0:T(8,128)} %get-tuple-element.26.space_ref) | copy-start | bytes 4718596
  244.6 60.6 %all-to-all-start.3 = ((bf16[64,224,128]{2,1,0:T(8,128)(2,1)}), bf16[64,224,128]{2,1,0:T(8,128)(2,1)}, u32[]{:S(2)}, u32[]{:S(2)}) async-start(bf16[64,224,128]{2,1,0:T(8,128)(2,1)} %add_parts.1), calls=%async_computation.3 | async-start | bytes 7340032 | tf_op jit(solution)/shard_map/all_to_all | solution.py:495
  255.6 55.4 %copy-start.1 = (bf16[1536,288]{0,1:T(8,128)(2,1)S(1)}, bf16[1536,288]{0,1:T(8,128)(2,1)}, u32[]{:S(2)}) copy-start(bf16[1536,288]{0,1:T(8,128)(2,1)} %param.21) | copy-start | bytes 2654212
Sparse Core Ops, SparseCore 0:
  10.4 75.5 all-gather.1
